TPU v7x, 32 devices: a whole 2x2x4 slice. The times are simulated.
32 devices in a mesh: row: 8 (over z, core), col: 4 (over y, x).
Axes of the slice: x: 2, y: 2, z: 4, core: 2. Of those that a mesh axis runs over, the one named last changes fastest.
Arguments:
- inv_top: float32 [2, 4096, 4096], P(None, 'row', 'col'), may hold values from -0.0625 to 0.0625
- inv_bottom: float32 [2, 4096, 4096], P(None, 'row', 'col'), may hold values from -0.0625 to 0.0625
- lower_panel: float32 [2, 4096, 4096], P(None, 'row', 'col'), may hold values from -0.0625 to 0.0625
- rhs_top: float32 [2, 4096, 128], P(None, 'col'), may hold values from -6 to 6
- rhs_bottom: float32 [2, 4096, 128], P(None, 'row'), may hold values from -6 to 6
- source_xy: float32 [2, 2, 4096], P(None, None, 'col'), may hold values from -20 to 20
- source_depth: float32 [2, 4096], P(None, 'col'), may hold values from -2 to -0.5
- body_label: int32 [2, 4096], P(None, 'col'), may hold values 0 or 1
- field_xy: float32 [2, 24576], P(None, 'row'), may hold values from -20 to 20
- region_label: int32 [24576], P('row'), may hold values 0 or 1
- lid_table: float32 [2, 2], replicated, may hold values from 0.3 to 3
- wave_number: float32 [1], replicated, may hold values from 0.5 to 1.5
Outputs:
- strengths: float32 [2, 2, 4096, 128], P(None, None, 'col')
- elevation: float32 [24576, 2, 128], P(('row', 'col'))
All inputs are finite; a program needn't handle non-finite values. No bound on the sum of `body_label` or of `region_label` on one device may be relied on, other than what follows from the above.
Results may differ from a plain program's by a relative error of at most 0.004.
Values sent between devices are 32-bit elements; how exact they have to be, the bound alone decides.
A program may use at most 64 MiB of HBM per device.

v0:
```python
import functools
import math

import jax
import jax.numpy as jnp
from jax import lax
from jax.experimental import pallas as pl
from jax.experimental.pallas import tpu as pltpu
from jax.sharding import PartitionSpec as P

SINE = (4.4428679, -7.30744342, 3.59478806, -0.78437397)
COSINE = (1.4142135, -6.97885099, 5.73946117, -1.88356297, 0.31069815)
GROUP = 32
CHUNK = 256


def polynomial(coefficients, value):
    total = coefficients[-1]
    for coefficient in coefficients[-2::-1]:
        total = total * value + coefficient
    return total


def green_kernel(points_ref, sources_ref, real_ref, imag_ref):
    def group(index, carry):
        rows = pl.ds(pl.multiple_of(index * GROUP, GROUP), GROUP)
        point = points_ref[rows, :]
        wide = (GROUP, CHUNK)
        point_x = jnp.broadcast_to(point[:, 0:1], wide)
        point_y = jnp.broadcast_to(point[:, 1:2], wide)
        second = jnp.broadcast_to(point[:, 2:3], wide) > 0.5
        for first in range(0, sources_ref.shape[1], CHUNK):
            lanes = slice(first, first + CHUNK)

            def source(row):
                return jnp.broadcast_to(sources_ref[row : row + 1, lanes], wide)

            delta_x = point_x - source(0)
            delta_y = point_y - source(1)
            square = delta_x * delta_x + delta_y * delta_y + source(2)
            inverse = lax.rsqrt(square)
            turns = square * inverse
            amplitude = jnp.where(second, source(4), source(3)) * inverse
            part = turns - jnp.round(turns)
            part_square = part * part
            half_sine = part * polynomial(SINE, part_square)
            half_cosine = polynomial(COSINE, part_square)
            scaled = amplitude * half_sine
            real_ref[rows, lanes] = (amplitude - scaled * half_sine).astype(jnp.bfloat16)
            imag_ref[rows, lanes] = (scaled * half_cosine).astype(jnp.bfloat16)
        return carry

    lax.fori_loop(0, points_ref.shape[0] // GROUP, group, 0)


def green_tiles(points, sources):
    point_count, source_count = points.shape[0], sources.shape[1]
    tile = max(t for t in range(GROUP, 257, GROUP) if point_count % t == 0)
    shape = jax.ShapeDtypeStruct((point_count, source_count), jnp.bfloat16)
    entries = point_count * source_count
    return pl.pallas_call(
        green_kernel,
        grid=(point_count // tile,),
        in_specs=[
            pl.BlockSpec((tile, points.shape[1]), lambda i: (i, 0)),
            pl.BlockSpec(sources.shape, lambda i: (0, 0)),
        ],
        out_specs=[pl.BlockSpec((tile, source_count), lambda i: (i, 0))] * 2,
        out_shape=[shape, shape],
        cost_estimate=pl.CostEstimate(
            flops=entries * 4000, bytes_accessed=entries * 4, transcendentals=entries
        ),
        compiler_params=pltpu.CompilerParams(vmem_limit_bytes=24 * 2**20),
    )(points, sources)


def turned(vector):
    count = vector.shape[-1] // 2
    return jnp.concatenate([-vector[:, count:], vector[:, :count]], axis=1)


def per_device(
    inv_top,
    inv_bottom,
    lower_panel,
    rhs_top,
    rhs_bottom,
    source_xy,
    source_depth,
    body_label,
    field_xy,
    region_label,
    lid_table,
    wave_number,
):
    col_rows, right_count = rhs_top.shape[1:]
    col_size = lax.axis_size("col")
    col_index = lax.axis_index("col")

    def product(matrix, vector):
        dot = functools.partial(
            jnp.dot, precision=lax.Precision.HIGH, preferred_element_type=jnp.float32
        )
        return dot(matrix[0], vector) + dot(matrix[1], turned(vector))

    def total_piece(partial_sum):
        return lax.psum_scatter(partial_sum, "col", scatter_dimension=0, tiled=True)

    def whole(piece):
        return lax.all_gather(piece, ("row", "col"), axis=0, tiled=True)

    def own_columns(full):
        return lax.dynamic_slice_in_dim(full, col_index * col_rows, col_rows, 0)

    def flat(pair):
        return jnp.concatenate([pair[0], pair[1]], axis=1)

    wave_value = wave_number[0]
    kappa = wave_value * (0.5 / math.pi)
    decay = kappa * jnp.exp(wave_value * source_depth)
    factors = [
        jnp.where(body_label == 1, lid_table[g, 1], lid_table[g, 0]) * decay for g in range(2)
    ]
    zero = jnp.zeros_like(decay)
    depth_turns = kappa * source_depth
    rows = jnp.stack(
        [
            kappa * source_xy[0],
            kappa * source_xy[1],
            depth_turns * depth_turns,
            factors[0],
            factors[1],
            zero,
            zero,
            zero,
        ]
    )
    rows = lax.all_gather(rows, "col", axis=2, tiled=True)
    out_rows = field_xy.shape[1] // col_size
    start = col_index * out_rows
    point_xy = kappa * lax.dynamic_slice_in_dim(field_xy, start, out_rows, 1)
    region = lax.dynamic_slice_in_dim(region_label, start, out_rows, 0).astype(jnp.float32)
    filler = jnp.zeros((5, out_rows), jnp.float32)
    points = jnp.concatenate([point_xy, region[None], filler]).T

    order = rows.shape[2]
    half = order // 2
    tiles = [
        [green_tiles(points, rows[:, b, h * half : (h + 1) * half]) for h in range(2)]
        for b in range(2)
    ]

    def term(block, full):
        weights = full.astype(jnp.bfloat16)
        crossed = turned(weights)
        total = 0.0
        for h in range(2):
            part = slice(h * half, (h + 1) * half)
            real, imag = tiles[block][h]
            total = total + jnp.dot(real, weights[part], preferred_element_type=jnp.float32)
            total = total + jnp.dot(imag, crossed[part], preferred_element_type=jnp.float32)
        return total

    top_full = whole(total_piece(product(inv_top, flat(rhs_top))))
    top_solved = own_columns(top_full)
    panel_piece = total_piece(product(lower_panel, top_solved))
    piece_rows = panel_piece.shape[0]
    rhs_piece = flat(lax.dynamic_slice_in_dim(rhs_bottom, col_index * piece_rows, piece_rows, 1))
    remainder = own_columns(whole(rhs_piece - panel_piece))
    bottom_full = whole(total_piece(product(inv_bottom, remainder)))
    bottom_solved = own_columns(bottom_full)

    elevation = term(0, top_full) + term(1, bottom_full)
    strengths = jnp.stack([top_solved, bottom_solved]).reshape(2, col_rows, 2, right_count)
    return (
        strengths.transpose(0, 2, 1, 3),
        elevation.reshape(out_rows, 2, right_count),
    )


def solution(mesh):
    in_specs = (
        P(None, "row", "col"),
        P(None, "row", "col"),
        P(None, "row", "col"),
        P(None, "col", None),
        P(None, "row", None),
        P(None, None, "col"),
        P(None, "col"),
        P(None, "col"),
        P(None, "row"),
        P("row"),
        P(),
        P(),
    )
    out_specs = (P(None, None, "col", None), P(("row", "col"), None, None))
    return jax.shard_map(
        per_device, mesh=mesh, in_specs=in_specs, out_specs=out_specs, check_vma=False
    )
```

profile of v0, /device:TPU:1, one launch (start us, length us, event | category | flops | bytes accessed | tf_op | source)
XLA Modules:
  0.0 344.1 jit_solution(16936582361741273385)
XLA Ops:
  7.2 1.4 slice_bitcast_fusion
  8.6 1.2 fusion.71
  9.9 3.6 %fusion.8 = f32[256,512]{1,0:T(8,128)S(1)} fusion(f32[2,512,1024]{2,1,0:T(8,128)} %param.12, f32[1024,128]{1,0:T(8,128)S(1)} %get-tuple-element.35, f32[1024,128]{1,0:T(8,128)S(1)} %fusion.71), kind=kOutput, calls=%fused_computation.13 | convolution fusion | flops 805568512 | bytes 3670016 | tf_op jit(solution)/shard_map/dot_general | solution.py:104
  13.5 2.7 fusion.22
  16.3 26.9 %reduce-scatter.4.cloned.1.call-done = f32[128,256]{0,1:T(8,128)} async-done(((f32[512,256]{0,1:T(8,128)}), f32[128,256]{0,1:T(8,128)}) %reduce-scatter.4.cloned.1.call-update) | async-done | bytes 131088 | tf_op jit(solution)/shard_map/reduce_scatter | solution.py:107
  43.2 70.3 %all-gather.4.cloned.1.call-done = f32[4096,256]{0,1:T(8,128)} async-done(((f32[128,256]{0,1:T(8,128)}), f32[4096,256]{0,1:T(8,128)}) %all-gather.4.cloned.1.call-update) | async-done | bytes 4194320 | tf_op jit(solution)/shard_map/all_gather | solution.py:110
  113.5 1.3 dynamic-slice_negate_fusion.1
  114.8 2.8 fusion.4
  117.6 1.3 constant_dynamic-slice_fusion.5
  119.0 1.0 copy-done.7
  120.0 1.9 fusion.28
  122.0 0.9 constant_dynamic-slice_fusion.2
  123.0 22.3 %reduce-scatter.6.cloned.1.call-done = f32[128,256]{0,1:T(8,128)} async-done(((f32[512,256]{0,1:T(8,128)}), f32[128,256]{0,1:T(8,128)}) %reduce-scatter.6.cloned.1.call-update) | async-done | bytes 131088 | tf_op jit(solution)/shard_map/reduce_scatter | solution.py:107
  145.4 1.6 maximum_subtract_fusion
  147.0 68.8 %all-gather.6.cloned.1.call-done = f32[4096,256]{0,1:T(8,128)} async-done(((f32[128,256]{0,1:T(8,128)}), f32[4096,256]{0,1:T(8,128)}) %all-gather.6.cloned.1.call-update) | async-done | bytes 4194320 | tf_op jit(solution)/shard_map/all_gather | solution.py:110
  215.8 1.4 dynamic-slice_negate_fusion
  217.2 2.8 fusion
  220.1 3.2 fusion.34
  223.3 23.4 %reduce-scatter.8.cloned.1.call-done = f32[128,256]{0,1:T(8,128)} async-done(((f32[512,256]{0,1:T(8,128)}), f32[128,256]{0,1:T(8,128)}) %reduce-scatter.8.cloned.1.call-update) | async-done | bytes 131088 | tf_op jit(solution)/shard_map/reduce_scatter | solution.py:107
  246.8 0.8 dynamic-slice_convert_fusion
  248.3 0.7 dynamic-slice_multiply_fusion
  249.1 0.2 copy.45
  249.3 0.7 fusion.74
  250.0 2.4 select_multiply_fusion
  252.6 7.1 %all_gather.15 = f32[8,2,4096]{2,0,1:T(8,128)S(1)} all-gather(f32[8,2,1024]{2,0,1:T(8,128)S(1)} %stack.33), channel_id=1, replica_groups=mesh['row'=8,'col'=4] {'col'}, dimensions={2}, use_global_device_ids=true | all-gather | bytes 327680 | tf_op jit(solution)/shard_map/all_gather | solution.py:138
  259.7 8.7 %shard_map.131 = (bf16[768,2048]{1,0:T(8,128)(2,1)S(1)}, bf16[768,2048]{1,0:T(8,128)(2,1)S(1)}) custom-call(f32[768,8]{1,0:T(8,128)S(1)} %bitcast.78, f32[8,2048]{1,0:T(8,128)S(1)} %get-tuple-element.41.sources_ref), custom_call_target="tpu_custom_call" | custom-call | flops 6291456000 | bytes 6291456 | tf_op jit(solution)/shard_map/pallas_call | solution.py:61
  268.4 8.7 %shard_map.132 = (bf16[768,2048]{1,0:T(8,128)(2,1)S(1)}, bf16[768,2048]{1,0:T(8,128)(2,1)S(1)}) custom-call(f32[768,8]{1,0:T(8,128)S(1)} %bitcast.79, f32[8,2048]{1,0:T(8,128)S(1)} %get-tuple-element.40.sources_ref), custom_call_target="tpu_custom_call" | custom-call | flops 6291456000 | bytes 6291456 | tf_op jit(solution)/shard_map/pallas_call | solution.py:61
  277.1 8.7 %shard_map.133 = (bf16[768,2048]{1,0:T(8,128)(2,1)S(1)}, bf16[768,2048]{1,0:T(8,128)(2,1)S(1)}) custom-call(f32[768,8]{1,0:T(8,128)S(1)} %bitcast.80, f32[8,2048]{1,0:T(8,128)S(1)} %get-tuple-element.39.sources_ref), custom_call_target="tpu_custom_call" | custom-call | flops 6291456000 | bytes 6291456 | tf_op jit(solution)/shard_map/pallas_call | solution.py:61
  285.9 1.6 copy-done.4
  287.5 8.7 %shard_map.134 = (bf16[768,2048]{1,0:T(8,128)(2,1)S(1)}, bf16[768,2048]{1,0:T(8,128)(2,1)S(1)}) custom-call(f32[768,8]{1,0:T(8,128)S(1)} %bitcast.81, f32[8,2048]{1,0:T(8,128)S(1)} %get-tuple-element.38.sources_ref), custom_call_target="tpu_custom_call" | custom-call | flops 6291456000 | bytes 6291456 | tf_op jit(solution)/shard_map/pallas_call | solution.py:61
  296.2 1.6 copy-done
  297.9 0.3 convert_element_type.10
  298.1 1.0 fusion.47
  299.3 1.0 convolution_add_fusion.5
  300.4 1.0 convolution_add_fusion.4
  301.4 1.9 convolution_add_fusion.3
  303.3 14.4 %all-gather.8.cloned.1.call-done = f32[4096,256]{0,1:T(8,128)} async-done(((f32[128,256]{0,1:T(8,128)}), f32[4096,256]{0,1:T(8,128)}) %all-gather.8.cloned.1.call-update) | async-done | bytes 4194320 | tf_op jit(solution)/shard_map/all_gather | solution.py:110
  317.7 1.3 constant_dynamic-slice_fusion.3
  319.0 2.8 maximum_bitcast_fusion
  321.7 2.9 copy.50
  324.6 2.5 convert_element_type.11
  327.3 1.7 copy-done.5
  329.0 1.1 fusion.43
  330.1 1.1 convolution_add_fusion.2
  331.2 0.8 copy-done.1
  332.0 1.1 convolution_add_fusion.1
  333.2 1.9 fusion.18
  335.1 2.1 copy.51
  (57 shorter events, 1.2 us)
Async XLA Ops:
  7.2 36.0 %reduce-scatter.4.cloned.1.call-start = ((), (), s32[]{:S(2)}) async-start(), calls=%async_computation.3 | async-start | bytes 655360 | tf_op jit(solution)/shard_map/reduce_scatter | solution.py:107
  7.2 6.2 %copy-start.8 = (f32[2,512,1024]{2,1,0:T(8,128)S(1)}, f32[2,512,1024]{2,1,0:T(8,128)}, u32[]{:S(2)}) copy-start(f32[2,512,1024]{2,1,0:T(8,128)} %param.12) | copy-start | bytes 12582916
  16.2 97.3 %all-gather.4.cloned.1.call-start = ((), (), s32[]{:S(2)}) async-start(), calls=%async_computation.4 | async-start | bytes 4325376 | tf_op jit(solution)/shard_map/all_gather | solution.py:110
  43.2 102.2 %reduce-scatter.6.cloned.1.call-start = ((), (), s32[]{:S(2)}) async-start(), calls=%async_computation.5 | async-start | bytes 655360 | tf_op jit(solution)/shard_map/reduce_scatter | solution.py:107
  114.8 5.1 %copy-start.9 = (f32[2,512,1024]{2,1,0:T(8,128)S(1)}, f32[2,512,1024]{2,1,0:T(8,128)}, u32[]{:S(2)}) copy-start(f32[2,512,1024]{2,1,0:T(8,128)} %param.14) | copy-start | bytes 12582916
  119.0 1.0 copy-start.7
  121.9 93.9 %all-gather.6.cloned.1.call-start = ((), (), s32[]{:S(2)}) async-start(), calls=%async_computation.6 | async-start | bytes 4325376 | tf_op jit(solution)/shard_map/all_gather | solution.py:110
  147.0 99.8 %reduce-scatter.8.cloned.1.call-start = ((), (), s32[]{:S(2)}) async-start(), calls=%async_computation.7 | async-start | bytes 655360 | tf_op jit(solution)/shard_map/reduce_scatter | solution.py:107
  215.8 4.2 %copy-start.10 = (f32[2,512,1024]{2,1,0:T(8,128)S(1)}, f32[2,512,1024]{2,1,0:T(8,128)}, u32[]{:S(2)}) copy-start(f32[2,512,1024]{2,1,0:T(8,128)} %param.13) | copy-start | bytes 12582916
  220.0 29.2 %copy-start.12 = (f32[2,2,1024]{2,1,0:T(2,128)S(1)}, f32[2,2,1024]{2,1,0:T(2,128)}, u32[]{:S(2)}) copy-start(f32[2,2,1024]{2,1,0:T(2,128)} %param.17) | copy-start | bytes 49156
  220.0 29.3 %copy-start.15 = (f32[2,2]{1,0:T(2,128)S(1)}, f32[2,2]{1,0:T(2,128)}, u32[]{:S(2)}) copy-start(f32[2,2]{1,0:T(2,128)} %param.22) | copy-start | bytes 52
  220.0 29.9 %copy-start.13 = (f32[2,1024]{1,0:T(2,128)S(1)}, f32[2,1024]{1,0:T(2,128)}, u32[]{:S(2)}) copy-start(f32[2,1024]{1,0:T(2,128)} %param.18) | copy-start | bytes 24580
  220.0 29.9 %copy-start.14 = (s32[2,1024]{1,0:T(2,128)S(1)}, s32[2,1024]{1,0:T(2,128)}, u32[]{:S(2)}) copy-start(s32[2,1024]{1,0:T(2,128)} %param.19) | copy-start | bytes 24580
  223.3 94.4 %all-gather.8.cloned.1.call-start = ((), (), s32[]{:S(2)}) async-start(), calls=%async_computation.8 | async-start | bytes 4325376 | tf_op jit(solution)/shard_map/all_gather | solution.py:110
  285.9 1.6 copy-start.4
  287.5 8.7 %copy-start.2 = (bf16[768,2048]{1,0:T(8,128)(2,1)}, bf16[768,2048]{1,0:T(8,128)(2,1)S(1)}, u32[]{:S(2)}) copy-start(bf16[768,2048]{1,0:T(8,128)(2,1)S(1)} %get-tuple-element.15) | copy-start | bytes 9437188
  287.5 10.4 %copy-start.6 = (f32[4096,256]{0,1:T(8,128)S(1)}, f32[4096,256]{0,1:T(8,128)}, u32[]{:S(2)}) copy-start(f32[4096,256]{0,1:T(8,128)} %all-gather.4.cloned.1.call-done) | copy-start | bytes 12582916
  296.2 1.6 copy-start
  327.1 1.9 copy-start.5
  327.3 2.9 copy-start.3
  330.1 1.9 copy-start.1
  332.0 1.2 copy-start.11
Sparse Core Ops, SparseCore 0:
  16.3 26.7 reduce-scatter.3
  46.5 67.0 all-gather.3
  122.0 23.2 reduce-scatter.5
  148.7 67.0 all-gather.5
  223.4 23.3 reduce-scatter.7
  249.9 67.7 all-gather.7
where the time goes:
time: 346 us; the launch traced here: 344 us
  waiting for transfers between devices  226 us (65%)
  Pallas kernels  34.9 us (10%)
  matrix products  27.3 us (8%)
  local copies, waits for them, and re-layouts  17.9 us (5%)
  other arithmetic  15.3 us (4%)
  between operations  15.2 us (4%)
  blocking collectives  7.06 us (2%)
    all_gather x3, waiting for transfers between devices, whole(): return lax.all_gather(piece, ('row', 'col'), axis=0, tiled=True)  153 us
    reduce_scatter x3, waiting for transfers between devices, total_piece(): return lax.psum_scatter(partial_sum, 'col', scatter_dimension=0, tiled=True)  72.6 us
    pallas_call x4, Pallas kernels, green_tiles(): pl.pallas_call(green_kernel, grid=(point_count // tile,), in_specs=[pl.Bl...  34.9 us
    dot_general x6, matrix products, product(): return dot(matrix[0], vector) + dot(matrix[1], turned(vector))  17 us
    unnamed x36, local copies, waits for them, and re-layouts  11.9 us
    all_gather x1, blocking collectives, per_device(): rows = lax.all_gather(rows, 'col', axis=2, tiled=True)  7.06 us
  transfers between devices with their start and end apart: 6, of which 6 were waited for; matrix products, arithmetic and copies ran while one was open for 3% of the time, Pallas kernels for 10%

commit v1 on v0

--- a/solution.py
+++ b/solution.py
@@ -74,6 +74,30 @@
     )(points, sources)
 
 
+def round_kernel(full_ref, weights_ref, crossed_ref):
+    count = full_ref.shape[1] // 2
+    real = full_ref[:, :count]
+    imag = full_ref[:, count:]
+    weights_ref[:, :count] = real.astype(jnp.bfloat16)
+    weights_ref[:, count:] = imag.astype(jnp.bfloat16)
+    crossed_ref[:, :count] = (-imag).astype(jnp.bfloat16)
+    crossed_ref[:, count:] = real.astype(jnp.bfloat16)
+
+
+def rounded(full):
+    tile = full.shape[0] // 4
+    shape = jax.ShapeDtypeStruct(full.shape, jnp.bfloat16)
+    spec = pl.BlockSpec((tile, full.shape[1]), lambda i: (i, 0))
+    return pl.pallas_call(
+        round_kernel,
+        grid=(4,),
+        in_specs=[spec],
+        out_specs=[spec, spec],
+        out_shape=[shape, shape],
+        compiler_params=pltpu.CompilerParams(vmem_limit_bytes=24 * 2**20),
+    )(full)
+
+
 def turned(vector):
     count = vector.shape[-1] // 2
     return jnp.concatenate([-vector[:, count:], vector[:, :count]], axis=1)
@@ -103,14 +127,61 @@
         )
         return dot(matrix[0], vector) + dot(matrix[1], turned(vector))
 
+    row_size = lax.axis_size("row")
+    row_index = lax.axis_index("row")
+    chips = row_size // 2
+    per_col = row_size // col_size
+    core = row_index % 2
+
+    def shift_col(piece, step):
+        pairs = [((i + step) % col_size, i) for i in range(col_size)]
+        return lax.ppermute(piece, "col", pairs)
+
+    def shift_chip(piece, step):
+        pairs = [((i + 2 * step) % row_size, i) for i in range(row_size)]
+        return lax.ppermute(piece, "row", pairs)
+
+    def sibling(piece):
+        return lax.ppermute(piece, "row", [(i, i ^ 1) for i in range(row_size)])
+
+    def by_core(mine, other, axis):
+        first = jnp.where(core == 0, mine, other)
+        second = jnp.where(core == 0, other, mine)
+        return jnp.stack([first, second], axis=axis)
+
     def total_piece(partial_sum):
-        return lax.psum_scatter(partial_sum, "col", scatter_dimension=0, tiled=True)
-
-    def whole(piece):
-        return lax.all_gather(piece, ("row", "col"), axis=0, tiled=True)
-
-    def own_columns(full):
-        return lax.dynamic_slice_in_dim(full, col_index * col_rows, col_rows, 0)
+        piece_rows = partial_sum.shape[0] // col_size
+
+        def piece_of(step):
+            place = (col_index - step + col_size) % col_size * piece_rows
+            return lax.dynamic_slice_in_dim(partial_sum, place, piece_rows, 0)
+
+        total = piece_of(0)
+        for step in range(1, col_size):
+            total = total + shift_col(piece_of(step), step)
+        return total
+
+    def columns(piece):
+        pairs = []
+        for r in range(row_size):
+            for c in range(col_size):
+                target = (r % per_col) * col_size + c
+                pairs.append((r * col_size + c, target * col_size + r // per_col))
+        piece = lax.ppermute(piece, ("row", "col"), pairs)
+        turned_list = [piece] + [shift_chip(piece, step) for step in range(1, chips)]
+        ring = jnp.stack(turned_list + turned_list)
+        chip = row_index // 2
+        mine = lax.dynamic_slice_in_dim(ring, (chips - chip) % chips, chips, 0)
+        return by_core(mine, sibling(mine), 1).reshape(-1, piece.shape[1])
+
+    def whole(own):
+        half_rows = own.shape[0] // 2
+        half = lax.dynamic_slice_in_dim(own, core * half_rows, half_rows, 0)
+        mine = [shift_col(half, step) for step in range(1, col_size)]
+        mine = jnp.stack(lax.optimization_barrier(mine))
+        mine, other = lax.optimization_barrier((mine, sibling(mine)))
+        rest = by_core(mine, other, 1).reshape(-1, own.shape[1])
+        return jnp.concatenate([own, rest])
 
     def flat(pair):
         return jnp.concatenate([pair[0], pair[1]], axis=1)
@@ -135,7 +206,9 @@
             zero,
         ]
     )
-    rows = lax.all_gather(rows, "col", axis=2, tiled=True)
+    rows = jnp.concatenate(
+        [rows] + [shift_col(rows, step) for step in range(1, col_size)], axis=2
+    )
     out_rows = field_xy.shape[1] // col_size
     start = col_index * out_rows
     point_xy = kappa * lax.dynamic_slice_in_dim(field_xy, start, out_rows, 1)
@@ -151,8 +224,7 @@
     ]
 
     def term(block, full):
-        weights = full.astype(jnp.bfloat16)
-        crossed = turned(weights)
+        weights, crossed = rounded(full)
         total = 0.0
         for h in range(2):
             part = slice(h * half, (h + 1) * half)
@@ -161,14 +233,14 @@
             total = total + jnp.dot(imag, crossed[part], preferred_element_type=jnp.float32)
         return total
 
-    top_full = whole(total_piece(product(inv_top, flat(rhs_top))))
-    top_solved = own_columns(top_full)
+    top_solved = columns(total_piece(product(inv_top, flat(rhs_top))))
+    top_full = whole(top_solved)
     panel_piece = total_piece(product(lower_panel, top_solved))
     piece_rows = panel_piece.shape[0]
     rhs_piece = flat(lax.dynamic_slice_in_dim(rhs_bottom, col_index * piece_rows, piece_rows, 1))
-    remainder = own_columns(whole(rhs_piece - panel_piece))
-    bottom_full = whole(total_piece(product(inv_bottom, remainder)))
-    bottom_solved = own_columns(bottom_full)
+    remainder = columns(rhs_piece - panel_piece)
+    bottom_solved = columns(total_piece(product(inv_bottom, remainder)))
+    bottom_full = whole(bottom_solved)
 
     elevation = term(0, top_full) + term(1, bottom_full)
     strengths = jnp.stack([top_solved, bottom_solved]).reshape(2, col_rows, 2, right_count)

time: 346 us -> 243 us (0.70)
  waiting for transfers between devices: 226 us -> 66.3 us
  starting transfers between devices: 0.24 us -> 54.1 us
  local copies, waits for them, and re-layouts: 17.9 us -> 36.1 us
  between operations: 15.2 us -> 2.25 us
  blocking collectives: 7.06 us -> 0 us
    all_gather x3 -> x0, waiting for transfers between devices: 153 us -> none  [whole(): return lax.all_gather(piece, ('row', 'col'), axis=0, tiled=True)]
    reduce_scatter x3 -> x0, waiting for transfers between devices: 72.6 us -> none  [total_piece(): return lax.psum_scatter(partial_sum, 'col', scatter_dimension=0, tiled=True)]
    ppermute x0 -> x35, waiting for transfers between devices: none -> 66.3 us  [the longest x9 32.4 us: shift_chip(): return lax.ppermute(piece, 'row', pairs)]
    ppermute x0 -> x35, starting transfers between devices: none -> 54.1 us  [the longest x18 18.1 us: shift_col(): return lax.ppermute(piece, 'col', pairs)]
    another operation x0 -> x10, local copies, waits for them, and re-layouts: none -> 9.45 us  [the longest x2 5.45 us: per_device(): jnp.stack([top_solved, bottom_solved]).reshape(2, col_rows, 2, right_count)]
    another operation x0 -> x12, other arithmetic: none -> 8.74 us  [the longest x10 5.99 us: by_core(): return jnp.stack([first, second], axis=axis)]
    unnamed x36 -> x68, local copies, waits for them, and re-layouts: 11.9 us -> 19.7 us
    all_gather x1 -> x0, blocking collectives: 7.06 us -> none  [per_device(): rows = lax.all_gather(rows, 'col', axis=2, tiled=True)]
  transfers between devices with their start and end apart: 6 -> 35, of which waited for: 6 -> 16; matrix products, arithmetic and copies ran while one was open for 3% -> 22% of each run, Pallas kernels for 10% -> 15%
where the time goes in v1:
time: 243 us; the launch traced here: 242 us
  waiting for transfers between devices  66.3 us (27%)
  starting transfers between devices  54.1 us (22%)
  Pallas kernels  36.4 us (15%)
  local copies, waits for them, and re-layouts  36.1 us (15%)
  matrix products  27.9 us (11%)
  other arithmetic  18.7 us (8%)
    pallas_call x4, Pallas kernels, green_tiles(): pl.pallas_call(green_kernel, grid=(point_count // tile,), in_specs=[pl.Bl...  34.8 us
    ppermute x9, waiting for transfers between devices, shift_chip(): return lax.ppermute(piece, 'row', pairs)  32.4 us
    ppermute x18, waiting for transfers between devices, shift_col(): return lax.ppermute(piece, 'col', pairs)  30.7 us
    unnamed x68, local copies, waits for them, and re-layouts  19.7 us
    dot_general x6, matrix products, product(): return dot(matrix[0], vector) + dot(matrix[1], turned(vector))  18.5 us
    ppermute x18, starting transfers between devices, shift_col(): return lax.ppermute(piece, 'col', pairs)  18.1 us
    ppermute x3, starting transfers between devices, columns(): piece = lax.ppermute(piece, ('row', 'col'), pairs)  15.4 us
    ppermute x9, starting transfers between devices, shift_chip(): return lax.ppermute(piece, 'row', pairs)  15.2 us
  transfers between devices with their start and end apart: 35, of which 16 were waited for; matrix products, arithmetic and copies ran while one was open for 22% of the time, Pallas kernels for 15%

profile of v1, /device:TPU:1, one launch (start us, length us, event | category | flops | bytes accessed | tf_op | source)
XLA Modules:
  0.0 241.7 jit_solution(1263808594783756811)
XLA Ops:
  3.5 3.3 %select_multiply_fusion = (f32[2,1024]{1,0:T(2,128)S(1)}, f32[1,2,1024]{2,1,0:T(2,128)S(1)}, f32[1,2,1024]{2,1,0:T(2,128)S(1)}) fusion(f32[]{:T(128)} %bitcast.50, f32[]{:T(128)} %bitcast.49, f32[2,1024]{1,0:T(2,128)} %param.18, f32[]{:T(128)} %bitcast.173, f32[]{:T(128)S(6)} %mul.81, s32[2,1024]{1,0:T(2,128)} %param.19, f32[]{:T(128)} %bitcast.47, f32[]{:T(128)} %bitcast.46), kind=kLoop, calls=%fused_computation.128 | loop fusion | flops 18432 | bytes 40984 | tf_op jit(solution)/shard_map/mul | solution.py:193
  7.0 3.0 %collective-permute-start.24 = (f32[8,2,1024]{2,0,1:T(8,128)S(1)}, f32[8,2,1024]{2,0,1:T(8,128)S(1)}, u32[]{:S(2)}, u32[]{:S(2)}) collective-permute-start(f32[8,2,1024]{2,0,1:T(8,128)S(1)} %stack.181), channel_id=1, source_target_pairs={{1,0},{2,1},{3,2},{0,3},{5,4},{6,5},{7,6},{4,7},{9,8},{10,9},{11,1... | collective-permute-start | bytes 196616 | tf_op jit(solution)/shard_map/ppermute | solution.py:138
  12.7 3.4 %fusion.8 = f32[256,512]{1,0:T(8,128)S(1)} fusion(f32[2,512,1024]{2,1,0:T(8,128)} %param.12, f32[1024,128]{1,0:T(8,128)S(1)} %get-tuple-element.69, f32[1024,128]{1,0:T(8,128)S(1)} %fusion.63), kind=kOutput, calls=%fused_computation.13 | convolution fusion | flops 805568512 | bytes 3670016 | tf_op jit(solution)/shard_map/dot_general | solution.py:128
  16.1 3.4 %fusion.19 = f32[256,512]{1,0:T(8,128)S(1)} fusion(f32[256,512]{1,0:T(8,128)S(1)} %fusion.8, f32[2,512,1024]{2,1,0:T(8,128)} %param.12, f32[1024,128]{1,0:T(8,128)S(1)} %get-tuple-element.68, f32[1024,128]{1,0:T(8,128)S(1)} %get-tuple-element.69), kind=kOutput, calls=%fused_computation.36 | convolution fusion | flops 805699584 | bytes 4194304 | tf_op jit(solution)/shard_map/dot_general | solution.py:128
  21.0 2.3 collective-permute-start
  27.5 6.1 %collective-permute-start.3 = (f32[128,256]{0,1:T(8,128)S(1)}, f32[128,256]{0,1:T(8,128)S(1)}, u32[]{:S(2)}, u32[]{:S(2)}) collective-permute-start(f32[128,256]{0,1:T(8,128)S(1)} %fusion.55), channel_id=1, source_target_pairs={{0,0},{1,4},{2,8},{3,12},{4,16},{5,20},{6,24},{7,28},{8,1},{9,5},{... | collective-permute-start | bytes 393224 | tf_op jit(solution)/shard_map/ppermute | solution.py:170
  33.6 1.9 collective-permute-done.3
  35.5 5.6 %collective-permute-start.4 = (f32[128,256]{0,1:T(8,128)S(1)}, f32[128,256]{0,1:T(8,128)S(1)}, u32[]{:S(2)}, u32[]{:S(2)}) collective-permute-start(f32[128,256]{0,1:T(8,128)S(1)} %collective-permute-done.3), channel_id=1, source_target_pairs={{8,0},{12,4},{16,8},{20,12},{24,16},{28,20},{0,24},{4,28},{9,1},{1... | collective-permute-start | bytes 393224 | tf_op jit(solution)/shard_map/ppermute | solution.py:142
  41.4 1.7 collective-permute-done.4
  43.1 8.2 %collective-permute-done.5 = f32[128,256]{0,1:T(8,128)S(1)} collective-permute-done((f32[128,256]{0,1:T(8,128)S(1)}, f32[128,256]{0,1:T(8,128)S(1)}, u32[]{:S(2)}, u32[]{:S(2)}) %collective-permute-start.5) | collective-permute-done | bytes 131104 | tf_op jit(solution)/shard_map/ppermute | solution.py:142
  53.1 8.7 %shard_map.131 = (bf16[768,2048]{1,0:T(8,128)(2,1)S(1)}, bf16[768,2048]{1,0:T(8,128)(2,1)S(1)}) custom-call(f32[768,8]{1,0:T(8,128)S(1)} %bitcast.174, f32[8,2048]{1,0:T(8,128)S(1)} %get-tuple-element.84.sources_ref), custom_call_target="tpu_custom_call" | custom-call | flops 6291456000 | bytes 6291456 | tf_op jit(solution)/shard_map/pallas_call | solution.py:61
  63.4 1.7 copy-done.5
  65.7 4.0 %fusion.4 = f32[256,512]{1,0:T(8,128)S(1)} fusion(f32[2,512,1024]{2,1,0:T(8,128)} %param.14, f32[1024,128]{1,0:T(8,128)S(1)} %get-tuple-element.65, f32[1024,128]{1,0:T(8,128)S(1)} %get-tuple-element.64), kind=kOutput, calls=%fused_computation.9 | convolution fusion | flops 805568512 | bytes 3670016 | tf_op jit(solution)/shard_map/dot_general | solution.py:128
  69.7 1.9 fusion.22
  74.3 3.5 %collective-permute-done.10 = f32[128,256]{0,1:T(8,128)S(1)} collective-permute-done((f32[128,256]{0,1:T(8,128)S(1)}, f32[128,256]{0,1:T(8,128)S(1)}, u32[]{:S(2)}, u32[]{:S(2)}) %collective-permute-start.10) | collective-permute-done | bytes 131104 | tf_op jit(solution)/shard_map/ppermute | solution.py:138
  77.9 2.2 collective-permute-done.9
  80.1 4.9 %collective-permute-start.11 = (f32[128,256]{0,1:T(8,128)S(1)}, f32[128,256]{0,1:T(8,128)S(1)}, u32[]{:S(2)}, u32[]{:S(2)}) collective-permute-start(f32[128,256]{0,1:T(8,128)S(1)} %maximum_subtract_fusion), channel_id=1, source_target_pairs={{0,0},{1,4},{2,8},{3,12},{4,16},{5,20},{6,24},{7,28},{8,1},{9,5},{... | collective-permute-start | bytes 393224 | tf_op jit(solution)/shard_map/ppermute | solution.py:170
  87.0 5.2 %collective-permute-start.12 = (f32[128,256]{0,1:T(8,128)S(1)}, f32[128,256]{0,1:T(8,128)S(1)}, u32[]{:S(2)}, u32[]{:S(2)}) collective-permute-start(f32[128,256]{0,1:T(8,128)S(1)} %collective-permute-done.11), channel_id=1, source_target_pairs={{8,0},{12,4},{16,8},{20,12},{24,16},{28,20},{0,24},{4,28},{9,1},{1... | collective-permute-start | bytes 393224 | tf_op jit(solution)/shard_map/ppermute | solution.py:142
  92.6 2.1 collective-permute-done.12
  94.7 8.8 %collective-permute-done.13 = f32[128,256]{0,1:T(8,128)S(1)} collective-permute-done((f32[128,256]{0,1:T(8,128)S(1)}, f32[128,256]{0,1:T(8,128)S(1)}, u32[]{:S(2)}, u32[]{:S(2)}) %collective-permute-start.13) | collective-permute-done | bytes 131104 | tf_op jit(solution)/shard_map/ppermute | solution.py:142
  104.8 8.7 %shard_map.133 = (bf16[768,2048]{1,0:T(8,128)(2,1)S(1)}, bf16[768,2048]{1,0:T(8,128)(2,1)S(1)}) custom-call(f32[768,8]{1,0:T(8,128)S(1)} %bitcast.175, f32[8,2048]{1,0:T(8,128)S(1)} %get-tuple-element.82.sources_ref), custom_call_target="tpu_custom_call" | custom-call | flops 6291456000 | bytes 6291456 | tf_op jit(solution)/shard_map/pallas_call | solution.py:61
  113.6 1.7 copy-done.7
  115.3 1.8 copy-done.9
  117.1 1.7 collective-permute-start.25
  119.8 3.7 %fusion = f32[256,512]{1,0:T(8,128)S(1)} fusion(f32[2,512,1024]{2,1,0:T(8,128)} %param.13, f32[1024,128]{1,0:T(8,128)S(1)} %get-tuple-element.61, f32[1024,128]{1,0:T(8,128)S(1)} %get-tuple-element.60), kind=kOutput, calls=%fused_computation.5 | convolution fusion | flops 805568512 | bytes 3670016 | tf_op jit(solution)/shard_map/dot_general | solution.py:128
  123.5 1.9 fusion.25
  125.6 2.3 collective-permute-start.18
  127.9 2.9 %collective-permute-done.25 = f32[512,256]{1,0:T(8,128)} collective-permute-done((f32[512,256]{1,0:T(8,128)S(1)}, f32[512,256]{1,0:T(8,128)}, u32[]{:S(2)}, u32[]{:S(2)}) %collective-permute-start.25) | collective-permute-done | bytes 524320 | tf_op jit(solution)/shard_map/ppermute | solution.py:138
  130.8 2.6 %collective-permute-start.16 = (f32[128,256]{0,1:T(8,128)S(1)}, f32[128,256]{0,1:T(8,128)S(1)}, u32[]{:S(2)}, u32[]{:S(2)}) collective-permute-start(f32[128,256]{0,1:T(8,128)S(1)} %get-tuple-element.70), channel_id=1, source_target_pairs={{1,0},{2,1},{3,2},{0,3},{5,4},{6,5},{7,6},{4,7},{9,8},{10,9},{11,1... | collective-permute-start | bytes 393224 | tf_op jit(solution)/shard_map/ppermute | solution.py:138
  133.4 8.7 %shard_map.134 = (bf16[768,2048]{1,0:T(8,128)(2,1)S(1)}, bf16[768,2048]{1,0:T(8,128)(2,1)S(1)}) custom-call(f32[768,8]{1,0:T(8,128)S(1)} %bitcast.176, f32[8,2048]{1,0:T(8,128)S(1)} %get-tuple-element.83.sources_ref), custom_call_target="tpu_custom_call" | custom-call | flops 6291456000 | bytes 6291456 | tf_op jit(solution)/shard_map/pallas_call | solution.py:61
  143.7 2.5 %collective-permute-done.26 = f32[512,256]{1,0:T(8,128)} collective-permute-done((f32[512,256]{1,0:T(8,128)S(1)}, f32[512,256]{1,0:T(8,128)}, u32[]{:S(2)}, u32[]{:S(2)}) %collective-permute-start.26) | collective-permute-done | bytes 524320 | tf_op jit(solution)/shard_map/ppermute | solution.py:138
  146.2 2.7 %collective-permute-done.17 = f32[128,256]{0,1:T(8,128)S(1)} collective-permute-done((f32[128,256]{0,1:T(8,128)S(1)}, f32[128,256]{0,1:T(8,128)S(1)}, u32[]{:S(2)}, u32[]{:S(2)}) %collective-permute-start.17) | collective-permute-done | bytes 131104 | tf_op jit(solution)/shard_map/ppermute | solution.py:138
  148.9 4.4 %collective-permute-start.19 = (f32[128,256]{0,1:T(8,128)S(1)}, f32[128,256]{0,1:T(8,128)S(1)}, u32[]{:S(2)}, u32[]{:S(2)}) collective-permute-start(f32[128,256]{0,1:T(8,128)S(1)} %fusion.51), channel_id=1, source_target_pairs={{0,0},{1,4},{2,8},{3,12},{4,16},{5,20},{6,24},{7,28},{8,1},{9,5},{... | collective-permute-start | bytes 393224 | tf_op jit(solution)/shard_map/ppermute | solution.py:170
  153.3 2.6 %pad_maximum_fusion.4 = f32[3,512,256]{2,1,0:T(8,128)} fusion(f32[1,512,256]{2,1,0:T(8,128)} %bitcast.54, f32[1,512,256]{2,1,0:T(8,128)} %bitcast.53, f32[1,512,256]{2,1,0:T(8,128)} %bitcast.52), kind=kLoop, calls=%fused_computation.23 | loop fusion | flops 786432 | bytes 3145728 | tf_op jit(solution)/shard_map/stack | solution.py:181
  156.0 3.5 %collective-permute-start.20 = (f32[128,256]{0,1:T(8,128)S(1)}, f32[128,256]{0,1:T(8,128)S(1)}, u32[]{:S(2)}, u32[]{:S(2)}) collective-permute-start(f32[128,256]{0,1:T(8,128)S(1)} %collective-permute-done.19), channel_id=1, source_target_pairs={{8,0},{12,4},{16,8},{20,12},{24,16},{28,20},{0,24},{4,28},{9,1},{1... | collective-permute-start | bytes 393224 | tf_op jit(solution)/shard_map/ppermute | solution.py:142
  159.8 2.1 collective-permute-done.20
  161.9 9.4 %collective-permute-done.21 = f32[128,256]{0,1:T(8,128)S(1)} collective-permute-done((f32[128,256]{0,1:T(8,128)S(1)}, f32[128,256]{0,1:T(8,128)S(1)}, u32[]{:S(2)}, u32[]{:S(2)}) %collective-permute-start.21) | collective-permute-done | bytes 131104 | tf_op jit(solution)/shard_map/ppermute | solution.py:142
  173.4 8.7 %shard_map.136 = (bf16[768,2048]{1,0:T(8,128)(2,1)S(1)}, bf16[768,2048]{1,0:T(8,128)(2,1)S(1)}) custom-call(f32[768,8]{1,0:T(8,128)S(1)} %bitcast.177, f32[8,2048]{1,0:T(8,128)S(1)} %copy-done), custom_call_target="tpu_custom_call" | custom-call | flops 6291456000 | bytes 6291456 | tf_op jit(solution)/shard_map/pallas_call | solution.py:61
  182.2 1.7 copy-done.13
  183.8 2.7 %stack.158 = f32[1,1024,2,128]{3,2,1,0:T(2,128)} reshape(f32[4,2,128,256]{3,2,1,0:T(8,128)} %copy-done.15) | data formatting | bytes 2097152 | tf_op jit(solution)/shard_map/stack | solution.py:246
  188.9 2.5 %copy.65 = f32[4,2,128,256]{3,2,1,0:T(8,128)} copy(f32[4,2,128,256]{2,3,0,1:T(8,128)} %pad_maximum_fusion.8) | data formatting | bytes 2097152 | tf_op jit(solution)/shard_map/stack | solution.py:150
  191.4 2.7 %stack.175 = f32[1,1024,2,128]{3,2,1,0:T(2,128)} reshape(f32[4,2,128,256]{3,2,1,0:T(8,128)} %copy.65) | data formatting | bytes 2097152 | tf_op jit(solution)/shard_map/stack | solution.py:246
  196.8 2.5 %maximum_bitcast_fusion = f32[2,2,1024,128]{3,1,2,0:T(2,128)S(1)} fusion(f32[1,1024,2,128]{3,2,1,0:T(2,128)} %stack.175, f32[1,1024,2,128]{3,2,1,0:T(2,128)} %stack.158), kind=kLoop, calls=%fused_computation.4 | loop fusion | flops 524288 | bytes 4194304 | tf_op jit(solution)/shard_map/transpose | solution.py:248
  200.7 2.2 select_bitcast_fusion.3
  203.8 4.8 %collective-permute-done.31 = f32[512,256]{1,0:T(8,128)S(1)} collective-permute-done((f32[512,256]{1,0:T(8,128)S(1)}, f32[512,256]{1,0:T(8,128)S(1)}, u32[]{:S(2)}, u32[]{:S(2)}) %collective-permute-start.31) | collective-permute-done | bytes 524320 | tf_op jit(solution)/shard_map/ppermute | solution.py:138
  208.6 10.9 %collective-permute-done.33 = f32[512,256]{1,0:T(8,128)S(1)} collective-permute-done((f32[512,256]{1,0:T(8,128)S(1)}, f32[512,256]{1,0:T(8,128)S(1)}, u32[]{:S(2)}, u32[]{:S(2)}) %collective-permute-start.33) | collective-permute-done | bytes 524320 | tf_op jit(solution)/shard_map/ppermute | solution.py:138
  237.6 2.0 fusion.18
  239.6 2.1 copy.75
  (172 shorter events, 50.9 us)
Async XLA Ops:
  7.0 26.6 %collective-permute-start.24 = (f32[8,2,1024]{2,0,1:T(8,128)S(1)}, f32[8,2,1024]{2,0,1:T(8,128)S(1)}, u32[]{:S(2)}, u32[]{:S(2)}) collective-permute-start(f32[8,2,1024]{2,0,1:T(8,128)S(1)} %stack.181), channel_id=1, source_target_pairs={{1,0},{2,1},{3,2},{0,3},{5,4},{6,5},{7,6},{4,7},{9,8},{10,9},{11,1... | collective-permute-start | bytes 196616 | tf_op jit(solution)/shard_map/ppermute | solution.py:138
  10.0 64.3 %collective-permute-start.29 = (f32[8,2,1024]{2,0,1:T(8,128)S(1)}, f32[8,2,1024]{2,0,1:T(8,128)S(1)}, u32[]{:S(2)}, u32[]{:S(2)}) collective-permute-start(f32[8,2,1024]{2,0,1:T(8,128)S(1)} %stack.181), channel_id=1, source_target_pairs={{2,0},{3,1},{0,2},{1,3},{6,4},{7,5},{4,6},{5,7},{10,8},{11,9},{8,1... | collective-permute-start | bytes 196616 | tf_op jit(solution)/shard_map/ppermute | solution.py:138
  19.6 6.6 %collective-permute-start.2 = (f32[128,256]{0,1:T(8,128)S(1)}, f32[128,256]{0,1:T(8,128)S(1)}, u32[]{:S(2)}, u32[]{:S(2)}) collective-permute-start(f32[128,256]{0,1:T(8,128)S(1)} %get-tuple-element.77), channel_id=1, source_target_pairs={{3,0},{0,1},{1,2},{2,3},{7,4},{4,5},{5,6},{6,7},{11,8},{8,9},{9,10... | collective-permute-start | bytes 393224 | tf_op jit(solution)/shard_map/ppermute | solution.py:138
  20.0 7.5 %collective-permute-start.1 = (f32[128,256]{0,1:T(8,128)S(1)}, f32[128,256]{0,1:T(8,128)S(1)}, u32[]{:S(2)}, u32[]{:S(2)}) collective-permute-start(f32[128,256]{0,1:T(8,128)S(1)} %get-tuple-element.78), channel_id=1, source_target_pairs={{2,0},{3,1},{0,2},{1,3},{6,4},{7,5},{4,6},{5,7},{10,8},{11,9},{8,1... | collective-permute-start | bytes 393224 | tf_op jit(solution)/shard_map/ppermute | solution.py:138
  21.0 6.5 %collective-permute-start = (f32[128,256]{0,1:T(8,128)S(1)}, f32[128,256]{0,1:T(8,128)S(1)}, u32[]{:S(2)}, u32[]{:S(2)}) collective-permute-start(f32[128,256]{0,1:T(8,128)S(1)} %get-tuple-element.76), channel_id=1, source_target_pairs={{1,0},{2,1},{3,2},{0,3},{5,4},{6,5},{7,6},{4,7},{9,8},{10,9},{11,1... | collective-permute-start | bytes 393224 | tf_op jit(solution)/shard_map/ppermute | solution.py:138
  26.2 48.1 %collective-permute-start.30 = (f32[8,2,1024]{2,0,1:T(8,128)S(1)}, f32[8,2,1024]{2,0,1:T(8,128)S(1)}, u32[]{:S(2)}, u32[]{:S(2)}) collective-permute-start(f32[8,2,1024]{2,0,1:T(8,128)S(1)} %stack.181), channel_id=1, source_target_pairs={{3,0},{0,1},{1,2},{2,3},{7,4},{4,5},{5,6},{6,7},{11,8},{8,9},{9,10... | collective-permute-start | bytes 196616 | tf_op jit(solution)/shard_map/ppermute | solution.py:138
  27.5 8.0 %collective-permute-start.3 = (f32[128,256]{0,1:T(8,128)S(1)}, f32[128,256]{0,1:T(8,128)S(1)}, u32[]{:S(2)}, u32[]{:S(2)}) collective-permute-start(f32[128,256]{0,1:T(8,128)S(1)} %fusion.55), channel_id=1, source_target_pairs={{0,0},{1,4},{2,8},{3,12},{4,16},{5,20},{6,24},{7,28},{8,1},{9,5},{... | collective-permute-start | bytes 393224 | tf_op jit(solution)/shard_map/ppermute | solution.py:170
  35.5 7.5 %collective-permute-start.4 = (f32[128,256]{0,1:T(8,128)S(1)}, f32[128,256]{0,1:T(8,128)S(1)}, u32[]{:S(2)}, u32[]{:S(2)}) collective-permute-start(f32[128,256]{0,1:T(8,128)S(1)} %collective-permute-done.3), channel_id=1, source_target_pairs={{8,0},{12,4},{16,8},{20,12},{24,16},{28,20},{0,24},{4,28},{9,1},{1... | collective-permute-start | bytes 393224 | tf_op jit(solution)/shard_map/ppermute | solution.py:142
  41.1 10.2 %collective-permute-start.5 = (f32[128,256]{0,1:T(8,128)S(1)}, f32[128,256]{0,1:T(8,128)S(1)}, u32[]{:S(2)}, u32[]{:S(2)}) collective-permute-start(f32[128,256]{0,1:T(8,128)S(1)} %collective-permute-done.3), channel_id=1, source_target_pairs={{16,0},{20,4},{24,8},{28,12},{0,16},{4,20},{8,24},{12,28},{17,1},{... | collective-permute-start | bytes 393224 | tf_op jit(solution)/shard_map/ppermute | solution.py:142
  41.1 10.2 %collective-permute-start.6 = (f32[128,256]{0,1:T(8,128)S(1)}, f32[128,256]{0,1:T(8,128)S(1)}, u32[]{:S(2)}, u32[]{:S(2)}) collective-permute-start(f32[128,256]{0,1:T(8,128)S(1)} %collective-permute-done.3), channel_id=1, source_target_pairs={{24,0},{28,4},{0,8},{4,12},{8,16},{12,20},{16,24},{20,28},{25,1},{... | collective-permute-start | bytes 393224 | tf_op jit(solution)/shard_map/ppermute | solution.py:142
  51.4 13.7 %collective-permute-start.7 = (f32[4,128,256]{1,2,0:T(8,128)S(1)}, f32[4,128,256]{1,2,0:T(8,128)S(1)}, u32[]{:S(2)}, u32[]{:S(2)}) collective-permute-start(f32[4,128,256]{1,2,0:T(8,128)S(1)} %constant_dynamic-slice_fusion.6), channel_id=1, source_target_pairs={{0,4},{4,0},{8,12},{12,8},{16,20},{20,16},{24,28},{28,24},{1,5},{5... | collective-permute-start | bytes 1572872 | tf_op jit(solution)/shard_map/ppermute | solution.py:145
  65.6 47.9 %copy-start.15 = (f32[4,2,128,256]{3,2,1,0:T(8,128)}, f32[4,2,128,256]{3,2,1,0:T(8,128)S(1)}, u32[]{:S(2)}) copy-start(f32[4,2,128,256]{3,2,1,0:T(8,128)S(1)} %copy.61) | copy-start | bytes 3145732
  65.6 4.1 %copy-start.18 = (f32[2,512,1024]{2,1,0:T(8,128)S(1)}, f32[2,512,1024]{2,1,0:T(8,128)}, u32[]{:S(2)}) copy-start(f32[2,512,1024]{2,1,0:T(8,128)} %param.14) | copy-start | bytes 12582916
  71.8 6.1 %collective-permute-start.10 = (f32[128,256]{0,1:T(8,128)S(1)}, f32[128,256]{0,1:T(8,128)S(1)}, u32[]{:S(2)}, u32[]{:S(2)}) collective-permute-start(f32[128,256]{0,1:T(8,128)S(1)} %get-tuple-element.74), channel_id=1, source_target_pairs={{3,0},{0,1},{1,2},{2,3},{7,4},{4,5},{5,6},{6,7},{11,8},{8,9},{9,10... | collective-permute-start | bytes 393224 | tf_op jit(solution)/shard_map/ppermute | solution.py:138
  72.3 7.8 %collective-permute-start.9 = (f32[128,256]{0,1:T(8,128)S(1)}, f32[128,256]{0,1:T(8,128)S(1)}, u32[]{:S(2)}, u32[]{:S(2)}) collective-permute-start(f32[128,256]{0,1:T(8,128)S(1)} %get-tuple-element.75), channel_id=1, source_target_pairs={{2,0},{3,1},{0,2},{1,3},{6,4},{7,5},{4,6},{5,7},{10,8},{11,9},{8,1... | collective-permute-start | bytes 393224 | tf_op jit(solution)/shard_map/ppermute | solution.py:138
  73.4 6.7 %collective-permute-start.8 = (f32[128,256]{0,1:T(8,128)S(1)}, f32[128,256]{0,1:T(8,128)S(1)}, u32[]{:S(2)}, u32[]{:S(2)}) collective-permute-start(f32[128,256]{0,1:T(8,128)S(1)} %get-tuple-element.73), channel_id=1, source_target_pairs={{1,0},{2,1},{3,2},{0,3},{5,4},{6,5},{7,6},{4,7},{9,8},{10,9},{11,1... | collective-permute-start | bytes 393224 | tf_op jit(solution)/shard_map/ppermute | solution.py:138
  80.1 6.9 %collective-permute-start.11 = (f32[128,256]{0,1:T(8,128)S(1)}, f32[128,256]{0,1:T(8,128)S(1)}, u32[]{:S(2)}, u32[]{:S(2)}) collective-permute-start(f32[128,256]{0,1:T(8,128)S(1)} %maximum_subtract_fusion), channel_id=1, source_target_pairs={{0,0},{1,4},{2,8},{3,12},{4,16},{5,20},{6,24},{7,28},{8,1},{9,5},{... | collective-permute-start | bytes 393224 | tf_op jit(solution)/shard_map/ppermute | solution.py:170
  87.0 7.7 %collective-permute-start.12 = (f32[128,256]{0,1:T(8,128)S(1)}, f32[128,256]{0,1:T(8,128)S(1)}, u32[]{:S(2)}, u32[]{:S(2)}) collective-permute-start(f32[128,256]{0,1:T(8,128)S(1)} %collective-permute-done.11), channel_id=1, source_target_pairs={{8,0},{12,4},{16,8},{20,12},{24,16},{28,20},{0,24},{4,28},{9,1},{1... | collective-permute-start | bytes 393224 | tf_op jit(solution)/shard_map/ppermute | solution.py:142
  92.3 11.3 %collective-permute-start.13 = (f32[128,256]{0,1:T(8,128)S(1)}, f32[128,256]{0,1:T(8,128)S(1)}, u32[]{:S(2)}, u32[]{:S(2)}) collective-permute-start(f32[128,256]{0,1:T(8,128)S(1)} %collective-permute-done.11), channel_id=1, source_target_pairs={{16,0},{20,4},{24,8},{28,12},{0,16},{4,20},{8,24},{12,28},{17,1},{... | collective-permute-start | bytes 393224 | tf_op jit(solution)/shard_map/ppermute | solution.py:142
  92.3 11.3 %collective-permute-start.14 = (f32[128,256]{0,1:T(8,128)S(1)}, f32[128,256]{0,1:T(8,128)S(1)}, u32[]{:S(2)}, u32[]{:S(2)}) collective-permute-start(f32[128,256]{0,1:T(8,128)S(1)} %collective-permute-done.11), channel_id=1, source_target_pairs={{24,0},{28,4},{0,8},{4,12},{8,16},{12,20},{16,24},{20,28},{25,1},{... | collective-permute-start | bytes 393224 | tf_op jit(solution)/shard_map/ppermute | solution.py:142
  103.7 15.5 %collective-permute-start.15 = (f32[4,128,256]{1,2,0:T(8,128)S(1)}, f32[4,128,256]{1,2,0:T(8,128)S(1)}, u32[]{:S(2)}, u32[]{:S(2)}) collective-permute-start(f32[4,128,256]{1,2,0:T(8,128)S(1)} %constant_dynamic-slice_fusion.4), channel_id=1, source_target_pairs={{0,4},{4,0},{8,12},{12,8},{16,20},{20,16},{24,28},{28,24},{1,5},{5... | collective-permute-start | bytes 1572872 | tf_op jit(solution)/shard_map/ppermute | solution.py:145
  117.1 13.7 %collective-permute-start.25 = (f32[512,256]{1,0:T(8,128)S(1)}, f32[512,256]{1,0:T(8,128)}, u32[]{:S(2)}, u32[]{:S(2)}) collective-permute-start(f32[512,256]{1,0:T(8,128)S(1)} %constant_dynamic-slice_fusion.2), channel_id=1, source_target_pairs={{1,0},{2,1},{3,2},{0,3},{5,4},{6,5},{7,6},{4,7},{9,8},{10,9},{11,1... | collective-permute-start | bytes 1572872 | tf_op jit(solution)/shard_map/ppermute | solution.py:138
  118.8 27.4 %collective-permute-start.26 = (f32[512,256]{1,0:T(8,128)S(1)}, f32[512,256]{1,0:T(8,128)}, u32[]{:S(2)}, u32[]{:S(2)}) collective-permute-start(f32[512,256]{1,0:T(8,128)S(1)} %constant_dynamic-slice_fusion.2), channel_id=1, source_target_pairs={{2,0},{3,1},{0,2},{1,3},{6,4},{7,5},{4,6},{5,7},{10,8},{11,9},{8,1... | collective-permute-start | bytes 1572872 | tf_op jit(solution)/shard_map/ppermute | solution.py:138
  118.8 27.4 %collective-permute-start.27 = (f32[512,256]{1,0:T(8,128)S(1)}, f32[512,256]{1,0:T(8,128)}, u32[]{:S(2)}, u32[]{:S(2)}) collective-permute-start(f32[512,256]{1,0:T(8,128)S(1)} %constant_dynamic-slice_fusion.2), channel_id=1, source_target_pairs={{3,0},{0,1},{1,2},{2,3},{7,4},{4,5},{5,6},{6,7},{11,8},{8,9},{9,10... | collective-permute-start | bytes 1572872 | tf_op jit(solution)/shard_map/ppermute | solution.py:138
  119.7 3.8 %copy-start.19 = (f32[2,512,1024]{2,1,0:T(8,128)S(1)}, f32[2,512,1024]{2,1,0:T(8,128)}, u32[]{:S(2)}) copy-start(f32[2,512,1024]{2,1,0:T(8,128)} %param.13) | copy-start | bytes 12582916
  125.6 20.6 %collective-permute-start.18 = (f32[128,256]{0,1:T(8,128)S(1)}, f32[128,256]{0,1:T(8,128)S(1)}, u32[]{:S(2)}, u32[]{:S(2)}) collective-permute-start(f32[128,256]{0,1:T(8,128)S(1)} %get-tuple-element.71), channel_id=1, source_target_pairs={{3,0},{0,1},{1,2},{2,3},{7,4},{4,5},{5,6},{6,7},{11,8},{8,9},{9,10... | collective-permute-start | bytes 393224 | tf_op jit(solution)/shard_map/ppermute | solution.py:138
  127.9 21.0 %collective-permute-start.17 = (f32[128,256]{0,1:T(8,128)S(1)}, f32[128,256]{0,1:T(8,128)S(1)}, u32[]{:S(2)}, u32[]{:S(2)}) collective-permute-start(f32[128,256]{0,1:T(8,128)S(1)} %get-tuple-element.72), channel_id=1, source_target_pairs={{2,0},{3,1},{0,2},{1,3},{6,4},{7,5},{4,6},{5,7},{10,8},{11,9},{8,1... | collective-permute-start | bytes 393224 | tf_op jit(solution)/shard_map/ppermute | solution.py:138
  130.8 18.1 %collective-permute-start.16 = (f32[128,256]{0,1:T(8,128)S(1)}, f32[128,256]{0,1:T(8,128)S(1)}, u32[]{:S(2)}, u32[]{:S(2)}) collective-permute-start(f32[128,256]{0,1:T(8,128)S(1)} %get-tuple-element.70), channel_id=1, source_target_pairs={{1,0},{2,1},{3,2},{0,3},{5,4},{6,5},{7,6},{4,7},{9,8},{10,9},{11,1... | collective-permute-start | bytes 393224 | tf_op jit(solution)/shard_map/ppermute | solution.py:138
  143.7 28.6 %copy-start.11 = (bf16[768,2048]{1,0:T(8,128)(2,1)}, bf16[768,2048]{1,0:T(8,128)(2,1)S(1)}, u32[]{:S(2)}) copy-start(bf16[768,2048]{1,0:T(8,128)(2,1)S(1)} %get-tuple-element.42) | copy-start | bytes 9437188
  148.9 7.1 %collective-permute-start.19 = (f32[128,256]{0,1:T(8,128)S(1)}, f32[128,256]{0,1:T(8,128)S(1)}, u32[]{:S(2)}, u32[]{:S(2)}) collective-permute-start(f32[128,256]{0,1:T(8,128)S(1)} %fusion.51), channel_id=1, source_target_pairs={{0,0},{1,4},{2,8},{3,12},{4,16},{5,20},{6,24},{7,28},{8,1},{9,5},{... | collective-permute-start | bytes 393224 | tf_op jit(solution)/shard_map/ppermute | solution.py:170
  153.3 20.1 %copy-start = (f32[8,2048]{1,0:T(8,128)S(1)}, f32[8,2048]{1,0:T(8,128)}, u32[]{:S(2)}) copy-start(f32[8,2048]{1,0:T(8,128)} %get-tuple-element.81.sources_ref) | copy-start | bytes 196612
  156.0 44.7 %collective-permute-start.28 = (f32[3,512,256]{2,1,0:T(8,128)}, f32[3,512,256]{2,1,0:T(8,128)}, u32[]{:S(2)}, u32[]{:S(2)}) collective-permute-start(f32[3,512,256]{2,1,0:T(8,128)} %pad_maximum_fusion.4), channel_id=1, source_target_pairs={{0,4},{4,0},{8,12},{12,8},{16,20},{20,16},{24,28},{28,24},{1,5},{5... | collective-permute-start | bytes 4718600 | tf_op jit(solution)/shard_map/ppermute | solution.py:145
  156.0 5.9 %collective-permute-start.20 = (f32[128,256]{0,1:T(8,128)S(1)}, f32[128,256]{0,1:T(8,128)S(1)}, u32[]{:S(2)}, u32[]{:S(2)}) collective-permute-start(f32[128,256]{0,1:T(8,128)S(1)} %collective-permute-done.19), channel_id=1, source_target_pairs={{8,0},{12,4},{16,8},{20,12},{24,16},{28,20},{0,24},{4,28},{9,1},{1... | collective-permute-start | bytes 393224 | tf_op jit(solution)/shard_map/ppermute | solution.py:142
  159.5 11.8 %collective-permute-start.21 = (f32[128,256]{0,1:T(8,128)S(1)}, f32[128,256]{0,1:T(8,128)S(1)}, u32[]{:S(2)}, u32[]{:S(2)}) collective-permute-start(f32[128,256]{0,1:T(8,128)S(1)} %collective-permute-done.19), channel_id=1, source_target_pairs={{16,0},{20,4},{24,8},{28,12},{0,16},{4,20},{8,24},{12,28},{17,1},{... | collective-permute-start | bytes 393224 | tf_op jit(solution)/shard_map/ppermute | solution.py:142
  159.5 11.8 %collective-permute-start.22 = (f32[128,256]{0,1:T(8,128)S(1)}, f32[128,256]{0,1:T(8,128)S(1)}, u32[]{:S(2)}, u32[]{:S(2)}) collective-permute-start(f32[128,256]{0,1:T(8,128)S(1)} %collective-permute-done.19), channel_id=1, source_target_pairs={{24,0},{28,4},{0,8},{4,12},{8,16},{12,20},{16,24},{20,28},{25,1},{... | collective-permute-start | bytes 393224 | tf_op jit(solution)/shard_map/ppermute | solution.py:142
  171.5 2.0 copy-start.20
  172.4 14.2 %collective-permute-start.23 = (f32[4,128,256]{1,2,0:T(8,128)}, f32[4,128,256]{1,2,0:T(8,128)}, u32[]{:S(2)}, u32[]{:S(2)}) collective-permute-start(f32[4,128,256]{1,2,0:T(8,128)} %constant_dynamic-slice_fusion.3), channel_id=1, source_target_pairs={{0,4},{4,0},{8,12},{12,8},{16,20},{20,16},{24,28},{28,24},{1,5},{5... | collective-permute-start | bytes 1572872 | tf_op jit(solution)/shard_map/ppermute | solution.py:145
  195.2 13.3 %collective-permute-start.31 = (f32[512,256]{1,0:T(8,128)S(1)}, f32[512,256]{1,0:T(8,128)S(1)}, u32[]{:S(2)}, u32[]{:S(2)}) collective-permute-start(f32[512,256]{1,0:T(8,128)S(1)} %constant_dynamic-slice_fusion.1), channel_id=1, source_target_pairs={{1,0},{2,1},{3,2},{0,3},{5,4},{6,5},{7,6},{4,7},{9,8},{10,9},{11,1... | collective-permute-start | bytes 1572872 | tf_op jit(solution)/shard_map/ppermute | solution.py:138
  195.3 13.2 %collective-permute-start.32 = (f32[512,256]{1,0:T(8,128)S(1)}, f32[512,256]{1,0:T(8,128)S(1)}, u32[]{:S(2)}, u32[]{:S(2)}) collective-permute-start(f32[512,256]{1,0:T(8,128)S(1)} %constant_dynamic-slice_fusion.1), channel_id=1, source_target_pairs={{2,0},{3,1},{0,2},{1,3},{6,4},{7,5},{4,6},{5,7},{10,8},{11,9},{8,1... | collective-permute-start | bytes 1572872 | tf_op jit(solution)/shard_map/ppermute | solution.py:138
  195.4 24.1 %collective-permute-start.33 = (f32[512,256]{1,0:T(8,128)S(1)}, f32[512,256]{1,0:T(8,128)S(1)}, u32[]{:S(2)}, u32[]{:S(2)}) collective-permute-start(f32[512,256]{1,0:T(8,128)S(1)} %constant_dynamic-slice_fusion.1), channel_id=1, source_target_pairs={{3,0},{0,1},{1,2},{2,3},{7,4},{4,5},{5,6},{6,7},{11,8},{8,9},{9,10... | collective-permute-start | bytes 1572872 | tf_op jit(solution)/shard_map/ppermute | solution.py:138
  203.7 17.4 %copy-start.16 = (f32[4,2,128,256]{3,2,1,0:T(8,128)S(1)}, f32[4,2,128,256]{3,2,1,0:T(8,128)}, u32[]{:S(2)}) copy-start(f32[4,2,128,256]{3,2,1,0:T(8,128)} %copy-done.15) | copy-start | bytes 3145732
  219.6 9.7 %collective-permute-start.34 = (f32[3,512,256]{2,1,0:T(8,128)S(1)}, f32[3,512,256]{2,1,0:T(8,128)S(1)}, u32[]{:S(2)}, u32[]{:S(2)}) collective-permute-start(f32[3,512,256]{2,1,0:T(8,128)S(1)} %pad_maximum_fusion.5), channel_id=1, source_target_pairs={{0,4},{4,0},{8,12},{12,8},{16,20},{20,16},{24,28},{28,24},{1,5},{5... | collective-permute-start | bytes 4718600 | tf_op jit(solution)/shard_map/ppermute | solution.py:145
  221.4 1.9 copy-start.2
  222.3 2.1 copy-start.6
  224.5 1.9 copy-start.10
  231.6 1.9 copy-start.4
  232.3 2.3 copy-start.12
  234.6 1.9 copy-start.14
  (8 other events, 13.2 us)

commit v2 on v1

--- a/solution.py
+++ b/solution.py
@@ -149,30 +149,27 @@
         second = jnp.where(core == 0, other, mine)
         return jnp.stack([first, second], axis=axis)
 
-    def total_piece(partial_sum):
+    def columns(partial_sum, block, half_index):
         piece_rows = partial_sum.shape[0] // col_size
-
-        def piece_of(step):
-            place = (col_index - step + col_size) % col_size * piece_rows
-            return lax.dynamic_slice_in_dim(partial_sum, place, piece_rows, 0)
-
-        total = piece_of(0)
-        for step in range(1, col_size):
-            total = total + shift_col(piece_of(step), step)
-        return total
-
-    def columns(piece):
-        pairs = []
-        for r in range(row_size):
-            for c in range(col_size):
-                target = (r % per_col) * col_size + c
-                pairs.append((r * col_size + c, target * col_size + r // per_col))
-        piece = lax.ppermute(piece, ("row", "col"), pairs)
-        turned_list = [piece] + [shift_chip(piece, step) for step in range(1, chips)]
+        total = 0.0
+        for step in range(col_size):
+            pairs = []
+            for r in range(row_size):
+                for c in range(col_size):
+                    target = (r % per_col) * col_size + (c + step) % col_size
+                    pairs.append((r * col_size + c, target * col_size + r // per_col))
+            place = (col_index + step) % col_size * piece_rows
+            piece = lax.dynamic_slice_in_dim(partial_sum, place, piece_rows, 0)
+            total = total + lax.ppermute(piece, ("row", "col"), pairs)
+        total, source_part = lax.optimization_barrier((total, sources_of(block, half_index)))
+        others = [shift_chip(total, step) for step in range(1, chips)]
+        others, tile = lax.optimization_barrier((others, green_tiles(points, source_part)))
+        tiles[block][half_index] = tile
+        turned_list = [total] + others
         ring = jnp.stack(turned_list + turned_list)
         chip = row_index // 2
         mine = lax.dynamic_slice_in_dim(ring, (chips - chip) % chips, chips, 0)
-        return by_core(mine, sibling(mine), 1).reshape(-1, piece.shape[1])
+        return by_core(mine, sibling(mine), 1).reshape(-1, total.shape[1])
 
     def whole(own):
         half_rows = own.shape[0] // 2
@@ -218,10 +215,10 @@
 
     order = rows.shape[2]
     half = order // 2
-    tiles = [
-        [green_tiles(points, rows[:, b, h * half : (h + 1) * half]) for h in range(2)]
-        for b in range(2)
-    ]
+    tiles = [[None, None], [None, None]]
+
+    def sources_of(block, half_index):
+        return rows[:, block, half_index * half : (half_index + 1) * half]
 
     def term(block, full):
         weights, crossed = rounded(full)
@@ -233,14 +230,18 @@
             total = total + jnp.dot(imag, crossed[part], preferred_element_type=jnp.float32)
         return total
 
-    top_solved = columns(total_piece(product(inv_top, flat(rhs_top))))
+    top_solved = columns(product(inv_top, flat(rhs_top)), 0, 0)
     top_full = whole(top_solved)
-    panel_piece = total_piece(product(lower_panel, top_solved))
-    piece_rows = panel_piece.shape[0]
-    rhs_piece = flat(lax.dynamic_slice_in_dim(rhs_bottom, col_index * piece_rows, piece_rows, 1))
-    remainder = columns(rhs_piece - panel_piece)
-    bottom_solved = columns(total_piece(product(inv_bottom, remainder)))
+    first_col = (col_index == 0).astype(jnp.float32)
+    panel_sum = first_col * flat(rhs_bottom) - product(lower_panel, top_solved)
+    remainder = columns(panel_sum, 0, 1)
+    bottom_solved = columns(product(inv_bottom, remainder), 1, 0)
+    bottom_solved, source_part = lax.optimization_barrier((bottom_solved, sources_of(1, 1)))
+    tiles[1][1] = green_tiles(points, source_part)
     bottom_full = whole(bottom_solved)
+    top_solved, bottom_solved, bottom_full, tiles[1][1] = lax.optimization_barrier(
+        (top_solved, bottom_solved, bottom_full, tiles[1][1])
+    )
 
     elevation = term(0, top_full) + term(1, bottom_full)
     strengths = jnp.stack([top_solved, bottom_solved]).reshape(2, col_rows, 2, right_count)

time: 243 us -> 236 us (0.971)
  waiting for transfers between devices: 66.3 us -> 23.4 us
  starting transfers between devices: 54.1 us -> 77.9 us
  other arithmetic: 18.7 us -> 24.1 us
  local copies, waits for them, and re-layouts: 36.1 us -> 40.3 us
    ppermute x9, waiting for transfers between devices: 32.4 us -> 0.02 us  [shift_chip(): return lax.ppermute(piece, 'row', pairs)]
    ppermute x3 -> x12, starting transfers between devices: 15.4 us -> 45.3 us  [columns(): total = total + lax.ppermute(piece, ('row', 'col'), pairs)]
    ppermute x18 -> x9, waiting for transfers between devices: 30.7 us -> 17.2 us  [shift_col(): return lax.ppermute(piece, 'col', pairs)]
    ppermute x18 -> x9, starting transfers between devices: 18.1 us -> 13.1 us  [shift_col(): return lax.ppermute(piece, 'col', pairs)]
    another operation x2 -> x4, local copies, waits for them, and re-layouts: 5.45 us -> 10.1 us  [per_device(): jnp.stack([top_solved, bottom_solved]).reshape(2, col_rows, 2, right_count)]
    another operation x10, other arithmetic: 5.99 us -> 9.12 us  [by_core(): return jnp.stack([first, second], axis=axis)]
    ppermute x3 -> x12, waiting for transfers between devices: 3.2 us -> 6.14 us  [columns(): total = total + lax.ppermute(piece, ('row', 'col'), pairs)]
    unnamed x68 -> x89, local copies, waits for them, and re-layouts: 19.7 us -> 19.4 us
  transfers between devices with their start and end apart: 35 -> 35, of which waited for: 16 -> 6; matrix products, arithmetic and copies ran while one was open for 22% -> 18% of each run, Pallas kernels for 15% -> 15%
where the time goes in v2:
time: 236 us; the launch traced here: 234 us
  starting transfers between devices  77.9 us (33%)
  local copies, waits for them, and re-layouts  40.3 us (17%)
  Pallas kernels  36.4 us (15%)
  matrix products  29.8 us (13%)
  other arithmetic  24.1 us (10%)
  waiting for transfers between devices  23.4 us (10%)
  between operations  2.4 us (1%)
    ppermute x12, starting transfers between devices, columns(): total = total + lax.ppermute(piece, ('row', 'col'), pairs)  45.3 us
    pallas_call x4, Pallas kernels, green_tiles(): pl.pallas_call(green_kernel, grid=(point_count // tile,), in_specs=[pl.Bl...  34.8 us
    unnamed x89, local copies, waits for them, and re-layouts  19.4 us
    dot_general x6, matrix products, product(): return dot(matrix[0], vector) + dot(matrix[1], turned(vector))  18.5 us
    ppermute x9, waiting for transfers between devices, shift_col(): return lax.ppermute(piece, 'col', pairs)  17.2 us
    ppermute x9, starting transfers between devices, shift_chip(): return lax.ppermute(piece, 'row', pairs)  15.7 us
    ppermute x9, starting transfers between devices, shift_col(): return lax.ppermute(piece, 'col', pairs)  13.1 us
    another operation x4, local copies, waits for them, and re-layouts, per_device(): jnp.stack([top_solved, bottom_solved]).reshape(2, col_rows, 2, right_count)  10.1 us
  transfers between devices with their start and end apart: 35, of which 6 were waited for; matrix products, arithmetic and copies ran while one was open for 18% of the time, Pallas kernels for 15%

profile of v2, /device:TPU:1, one launch (start us, length us, event | category | flops | bytes accessed | tf_op | source)
XLA Modules:
  0.0 234.3 jit_solution(14831129604237597106)
XLA Ops:
  3.5 3.2 %select_multiply_fusion = (f32[2,1024]{1,0:T(2,128)S(1)}, f32[1,2,1024]{2,1,0:T(2,128)S(1)}, f32[1,2,1024]{2,1,0:T(2,128)S(1)}) fusion(f32[]{:T(128)} %bitcast.14, f32[]{:T(128)} %bitcast.13, f32[2,1024]{1,0:T(2,128)} %param.18, f32[]{:T(128)} %bitcast.155, f32[]{:T(128)S(6)} %mul.83, s32[2,1024]{1,0:T(2,128)} %param.19, f32[]{:T(128)} %bitcast.11, f32[]{:T(128)} %bitcast.10), kind=kLoop, calls=%fused_computation.126 | loop fusion | flops 18432 | bytes 40984 | tf_op jit(solution)/shard_map/mul | solution.py:190
  7.5 3.0 %collective-permute-start.4 = (f32[8,2,1024]{2,0,1:T(8,128)}, f32[8,2,1024]{2,0,1:T(8,128)S(1)}, u32[]{:S(2)}, u32[]{:S(2)}) collective-permute-start(f32[8,2,1024]{2,0,1:T(8,128)} %stack.156), channel_id=1, source_target_pairs={{1,0},{2,1},{3,2},{0,3},{5,4},{6,5},{7,6},{4,7},{9,8},{10,9},{11,1... | collective-permute-start | bytes 196616 | tf_op jit(solution)/shard_map/ppermute | solution.py:138
  12.9 3.4 %fusion.8 = f32[256,512]{1,0:T(8,128)S(1)} fusion(f32[2,512,1024]{2,1,0:T(8,128)} %param.12, f32[1024,128]{1,0:T(8,128)S(1)} %get-tuple-element.125, f32[1024,128]{1,0:T(8,128)S(1)} %fusion.69), kind=kOutput, calls=%fused_computation.13 | convolution fusion | flops 805568512 | bytes 3670016 | tf_op jit(solution)/shard_map/dot_general | solution.py:128
  16.4 3.4 %fusion.22 = f32[256,512]{1,0:T(8,128)S(1)} fusion(f32[256,512]{1,0:T(8,128)S(1)} %fusion.8, f32[2,512,1024]{2,1,0:T(8,128)} %param.12, f32[1024,128]{1,0:T(8,128)S(1)} %get-tuple-element.124, f32[1024,128]{1,0:T(8,128)S(1)} %get-tuple-element.125), kind=kOutput, calls=%fused_computation.36 | convolution fusion | flops 805699584 | bytes 4194304 | tf_op jit(solution)/shard_map/dot_general | solution.py:128
  19.9 4.2 %collective-permute-start.1 = (f32[128,256]{0,1:T(8,128)S(1)}, f32[128,256]{0,1:T(8,128)S(1)}, u32[]{:S(2)}, u32[]{:S(2)}) collective-permute-start(f32[128,256]{0,1:T(8,128)S(1)} %get-tuple-element.136), channel_id=1, source_target_pairs={{0,4},{1,8},{2,12},{3,0},{4,20},{5,24},{6,28},{7,16},{8,5},{9,9},{... | collective-permute-start | bytes 393224 | tf_op jit(solution)/shard_map/ppermute | solution.py:163
  24.1 3.1 %collective-permute-start.3 = (f32[128,256]{0,1:T(8,128)S(1)}, f32[128,256]{0,1:T(8,128)S(1)}, u32[]{:S(2)}, u32[]{:S(2)}) collective-permute-start(f32[128,256]{0,1:T(8,128)S(1)} %get-tuple-element.137), channel_id=1, source_target_pairs={{0,12},{1,0},{2,4},{3,8},{4,28},{5,16},{6,20},{7,24},{8,13},{9,1},... | collective-permute-start | bytes 393224 | tf_op jit(solution)/shard_map/ppermute | solution.py:163
  27.2 2.3 collective-permute-start.2
  29.5 5.4 %collective-permute-start = (f32[128,256]{0,1:T(8,128)S(1)}, f32[128,256]{0,1:T(8,128)S(1)}, u32[]{:S(2)}, u32[]{:S(2)}) collective-permute-start(f32[128,256]{0,1:T(8,128)S(1)} %get-tuple-element.139), channel_id=1, source_target_pairs={{0,0},{1,4},{2,8},{3,12},{4,16},{5,20},{6,24},{7,28},{8,1},{9,5},{... | collective-permute-start | bytes 393224 | tf_op jit(solution)/shard_map/ppermute | solution.py:163
  40.3 2.3 collective-permute-start.5
  42.5 8.7 %shard_map.131 = (bf16[768,2048]{1,0:T(8,128)(2,1)S(1)}, bf16[768,2048]{1,0:T(8,128)(2,1)S(1)}) custom-call(f32[768,8]{1,0:T(8,128)S(1)} %bitcast.156, f32[8,2048]{1,0:T(8,128)S(1)} %get-tuple-element.53.sources_ref), custom_call_target="tpu_custom_call" | custom-call | flops 6291456000 | bytes 6291456 | tf_op jit(solution)/shard_map/pallas_call | solution.py:61
  56.0 2.4 %collective-permute-start.14 = (f32[8,2,1024]{2,0,1:T(8,128)}, f32[8,2,1024]{2,0,1:T(8,128)}, u32[]{:S(2)}, u32[]{:S(2)}) collective-permute-start(f32[8,2,1024]{2,0,1:T(8,128)} %stack.156), channel_id=1, source_target_pairs={{3,0},{0,1},{1,2},{2,3},{7,4},{4,5},{5,6},{6,7},{11,8},{8,9},{9,10... | collective-permute-start | bytes 196616 | tf_op jit(solution)/shard_map/ppermute | solution.py:138
  58.7 3.2 %collective-permute-done.13 = f32[8,2,1024]{2,0,1:T(8,128)} collective-permute-done((f32[8,2,1024]{2,0,1:T(8,128)}, f32[8,2,1024]{2,0,1:T(8,128)}, u32[]{:S(2)}, u32[]{:S(2)}) %collective-permute-start.13) | collective-permute-done | bytes 65568 | tf_op jit(solution)/shard_map/ppermute | solution.py:138
  65.9 4.0 %fusion.4 = f32[256,512]{1,0:T(8,128)S(1)} fusion(f32[2,512,1024]{2,1,0:T(8,128)} %param.14, f32[1024,128]{1,0:T(8,128)S(1)} %get-tuple-element.121, f32[1024,128]{1,0:T(8,128)S(1)} %get-tuple-element.120), kind=kOutput, calls=%fused_computation.9 | convolution fusion | flops 805568512 | bytes 3670016 | tf_op jit(solution)/shard_map/dot_general | solution.py:128
  69.9 2.0 fusion.31
  72.0 3.6 %collective-permute-start.10 = (f32[128,256]{0,1:T(8,128)S(1)}, f32[128,256]{0,1:T(8,128)S(1)}, u32[]{:S(2)}, u32[]{:S(2)}) collective-permute-start(f32[128,256]{0,1:T(8,128)S(1)} %get-tuple-element.130), channel_id=1, source_target_pairs={{0,4},{1,8},{2,12},{3,0},{4,20},{5,24},{6,28},{7,16},{8,5},{9,9},{... | collective-permute-start | bytes 393224 | tf_op jit(solution)/shard_map/ppermute | solution.py:163
  75.6 3.3 %collective-permute-start.12 = (f32[128,256]{0,1:T(8,128)S(1)}, f32[128,256]{0,1:T(8,128)S(1)}, u32[]{:S(2)}, u32[]{:S(2)}) collective-permute-start(f32[128,256]{0,1:T(8,128)S(1)} %get-tuple-element.131), channel_id=1, source_target_pairs={{0,12},{1,0},{2,4},{3,8},{4,28},{5,16},{6,20},{7,24},{8,13},{9,1},... | collective-permute-start | bytes 393224 | tf_op jit(solution)/shard_map/ppermute | solution.py:163
  79.0 3.5 %collective-permute-start.11 = (f32[128,256]{0,1:T(8,128)S(1)}, f32[128,256]{0,1:T(8,128)S(1)}, u32[]{:S(2)}, u32[]{:S(2)}) collective-permute-start(f32[128,256]{0,1:T(8,128)S(1)} %get-tuple-element.132), channel_id=1, source_target_pairs={{0,8},{1,12},{2,0},{3,4},{4,24},{5,28},{6,16},{7,20},{8,9},{9,13},... | collective-permute-start | bytes 393224 | tf_op jit(solution)/shard_map/ppermute | solution.py:163
  82.5 1.9 collective-permute-start.9
  85.1 4.2 %collective-permute-done.9 = f32[128,256]{0,1:T(8,128)S(1)} collective-permute-done((f32[128,256]{0,1:T(8,128)S(1)}, f32[128,256]{0,1:T(8,128)S(1)}, u32[]{:S(2)}, u32[]{:S(2)}) %collective-permute-start.9) | collective-permute-done | bytes 131104 | tf_op jit(solution)/shard_map/ppermute | solution.py:163
  89.4 3.3 %collective-permute-start.17 = (f32[128,256]{0,1:T(8,128)S(1)}, f32[128,256]{0,1:T(8,128)S(1)}, u32[]{:S(2)}, u32[]{:S(2)}) collective-permute-start(f32[128,256]{0,1:T(8,128)S(1)} %add_add_fusion.1), channel_id=1, source_target_pairs={{24,0},{28,4},{0,8},{4,12},{8,16},{12,20},{16,24},{20,28},{25,1},{... | collective-permute-start | bytes 393224 | tf_op jit(solution)/shard_map/ppermute | solution.py:142
  94.8 8.7 %shard_map.132 = (bf16[768,2048]{1,0:T(8,128)(2,1)S(1)}, bf16[768,2048]{1,0:T(8,128)(2,1)S(1)}) custom-call(f32[768,8]{1,0:T(8,128)S(1)} %bitcast.157, f32[8,2048]{1,0:T(8,128)S(1)} %get-tuple-element.60.sources_ref), custom_call_target="tpu_custom_call" | custom-call | flops 6291456000 | bytes 6291456 | tf_op jit(solution)/shard_map/pallas_call | solution.py:61
  103.5 1.7 copy-done.9
  107.3 2.3 collective-permute-start.33
  113.1 3.7 %fusion = f32[256,512]{1,0:T(8,128)S(1)} fusion(f32[2,512,1024]{2,1,0:T(8,128)} %param.13, f32[1024,128]{1,0:T(8,128)S(1)} %get-tuple-element.117, f32[1024,128]{1,0:T(8,128)S(1)} %get-tuple-element.116), kind=kOutput, calls=%fused_computation.5 | convolution fusion | flops 805568512 | bytes 3670016 | tf_op jit(solution)/shard_map/dot_general | solution.py:128
  116.8 1.9 fusion.34
  118.9 3.7 %collective-permute-start.20 = (f32[128,256]{0,1:T(8,128)S(1)}, f32[128,256]{0,1:T(8,128)S(1)}, u32[]{:S(2)}, u32[]{:S(2)}) collective-permute-start(f32[128,256]{0,1:T(8,128)S(1)} %get-tuple-element.126), channel_id=1, source_target_pairs={{0,4},{1,8},{2,12},{3,0},{4,20},{5,24},{6,28},{7,16},{8,5},{9,9},{... | collective-permute-start | bytes 393224 | tf_op jit(solution)/shard_map/ppermute | solution.py:163
  122.6 3.1 %collective-permute-start.22 = (f32[128,256]{0,1:T(8,128)S(1)}, f32[128,256]{0,1:T(8,128)S(1)}, u32[]{:S(2)}, u32[]{:S(2)}) collective-permute-start(f32[128,256]{0,1:T(8,128)S(1)} %get-tuple-element.127), channel_id=1, source_target_pairs={{0,12},{1,0},{2,4},{3,8},{4,28},{5,16},{6,20},{7,24},{8,13},{9,1},... | collective-permute-start | bytes 393224 | tf_op jit(solution)/shard_map/ppermute | solution.py:163
  125.7 3.4 %collective-permute-start.21 = (f32[128,256]{0,1:T(8,128)S(1)}, f32[128,256]{0,1:T(8,128)S(1)}, u32[]{:S(2)}, u32[]{:S(2)}) collective-permute-start(f32[128,256]{0,1:T(8,128)S(1)} %get-tuple-element.128), channel_id=1, source_target_pairs={{0,8},{1,12},{2,0},{3,4},{4,24},{5,28},{6,16},{7,20},{8,9},{9,13},... | collective-permute-start | bytes 393224 | tf_op jit(solution)/shard_map/ppermute | solution.py:163
  129.1 6.7 %collective-permute-done.32 = f32[512,256]{1,0:T(8,128)} collective-permute-done((f32[512,256]{1,0:T(8,128)S(1)}, f32[512,256]{1,0:T(8,128)}, u32[]{:S(2)}, u32[]{:S(2)}) %collective-permute-start.32) | collective-permute-done | bytes 524320 | tf_op jit(solution)/shard_map/ppermute | solution.py:138
  135.7 7.9 %collective-permute-start.19 = (f32[128,256]{0,1:T(8,128)S(1)}, f32[128,256]{0,1:T(8,128)S(1)}, u32[]{:S(2)}, u32[]{:S(2)}) collective-permute-start(f32[128,256]{0,1:T(8,128)S(1)} %get-tuple-element.129), channel_id=1, source_target_pairs={{0,0},{1,4},{2,8},{3,12},{4,16},{5,20},{6,24},{7,28},{8,1},{9,5},{... | collective-permute-start | bytes 393224 | tf_op jit(solution)/shard_map/ppermute | solution.py:163
  143.6 1.9 collective-permute-done.19
  145.5 3.1 %collective-permute-start.25 = (f32[128,256]{0,1:T(8,128)S(1)}, f32[128,256]{0,1:T(8,128)S(1)}, u32[]{:S(2)}, u32[]{:S(2)}) collective-permute-start(f32[128,256]{0,1:T(8,128)S(1)} %add_add_fusion), channel_id=1, source_target_pairs={{24,0},{28,4},{0,8},{4,12},{8,16},{12,20},{16,24},{20,28},{25,1},{... | collective-permute-start | bytes 393224 | tf_op jit(solution)/shard_map/ppermute | solution.py:142
  151.4 8.7 %shard_map.133 = (bf16[768,2048]{1,0:T(8,128)(2,1)S(1)}, bf16[768,2048]{1,0:T(8,128)(2,1)S(1)}) custom-call(f32[768,8]{1,0:T(8,128)S(1)} %bitcast.158, f32[8,2048]{1,0:T(8,128)S(1)} %copy-done.5), custom_call_target="tpu_custom_call" | custom-call | flops 6291456000 | bytes 6291456 | tf_op jit(solution)/shard_map/pallas_call | solution.py:61
  161.3 2.6 %pad_maximum_fusion.5 = f32[3,512,256]{2,1,0:T(8,128)} fusion(f32[1,512,256]{2,1,0:T(8,128)} %bitcast.61, f32[1,512,256]{2,1,0:T(8,128)} %bitcast.60, f32[1,512,256]{2,1,0:T(8,128)} %bitcast.59), kind=kLoop, calls=%fused_computation.24 | loop fusion | flops 786432 | bytes 3145728 | tf_op jit(solution)/shard_map/stack | solution.py:178
  165.9 2.5 %copy.73 = f32[4,2,128,256]{3,2,1,0:T(8,128)} copy(f32[4,2,128,256]{2,3,0,1:T(8,128)} %pad_maximum_fusion.8) | data formatting | bytes 2097152 | tf_op jit(solution)/shard_map/stack | solution.py:150
  170.7 2.3 collective-permute-start.27
  173.8 8.7 %shard_map.134 = (bf16[768,2048]{1,0:T(8,128)(2,1)S(1)}, bf16[768,2048]{1,0:T(8,128)(2,1)S(1)}) custom-call(f32[768,8]{1,0:T(8,128)S(1)} %bitcast.159, f32[8,2048]{1,0:T(8,128)S(1)} %copy-done.6), custom_call_target="tpu_custom_call" | custom-call | flops 6291456000 | bytes 6291456 | tf_op jit(solution)/shard_map/pallas_call | solution.py:61
  182.6 4.5 %select_bitcast_fusion.1 = (f32[3,1,512,256]{3,2,0,1:T(8,128)S(1)}, f32[3,1,512,256]{3,2,0,1:T(8,128)S(1)}) fusion(f32[3,512,256]{2,1,0:T(8,128)} %pad_maximum_fusion.5, f32[3,512,256]{2,1,0:T(8,128)} %collective-permute-done.34, pred[]{:T(512)S(6)} %eq.36), kind=kLoop, calls=%fused_computation.26 | loop fusion | flops 786432 | bytes 6291457 | tf_op jit(solution)/shard_map/stack | solution.py:150
  187.8 6.3 %collective-permute-done.28 = f32[512,256]{1,0:T(8,128)S(1)} collective-permute-done((f32[512,256]{1,0:T(8,128)S(1)}, f32[512,256]{1,0:T(8,128)S(1)}, u32[]{:S(2)}, u32[]{:S(2)}) %collective-permute-start.28) | collective-permute-done | bytes 524320 | tf_op jit(solution)/shard_map/ppermute | solution.py:138
  198.8 1.9 fusion.59
  200.8 1.9 fusion.55
  202.7 2.0 fusion.57
  206.7 2.3 pad_maximum_fusion.full_ref
  209.0 2.8 %stack.188 = f32[1,1024,2,128]{3,2,1,0:T(2,128)} reshape(f32[1024,256]{1,0:T(8,128)} %bitcast.163) | data formatting | bytes 2097152 | tf_op jit(solution)/shard_map/stack | solution.py:247
  211.8 2.3 copy.75
  214.0 2.7 %stack.189 = f32[1,1024,2,128]{3,2,1,0:T(2,128)} reshape(f32[1024,256]{1,0:T(8,128)} %bitcast.166) | data formatting | bytes 2097152 | tf_op jit(solution)/shard_map/stack | solution.py:247
  216.8 2.3 copy.76
  219.1 2.2 copy-done
  (195 shorter events, 57.3 us)
Async XLA Ops:
  7.5 29.1 %collective-permute-start.4 = (f32[8,2,1024]{2,0,1:T(8,128)}, f32[8,2,1024]{2,0,1:T(8,128)S(1)}, u32[]{:S(2)}, u32[]{:S(2)}) collective-permute-start(f32[8,2,1024]{2,0,1:T(8,128)} %stack.156), channel_id=1, source_target_pairs={{1,0},{2,1},{3,2},{0,3},{5,4},{6,5},{7,6},{4,7},{9,8},{10,9},{11,1... | collective-permute-start | bytes 196616 | tf_op jit(solution)/shard_map/ppermute | solution.py:138
  19.9 18.2 %collective-permute-start.1 = (f32[128,256]{0,1:T(8,128)S(1)}, f32[128,256]{0,1:T(8,128)S(1)}, u32[]{:S(2)}, u32[]{:S(2)}) collective-permute-start(f32[128,256]{0,1:T(8,128)S(1)} %get-tuple-element.136), channel_id=1, source_target_pairs={{0,4},{1,8},{2,12},{3,0},{4,20},{5,24},{6,28},{7,16},{8,5},{9,9},{... | collective-permute-start | bytes 393224 | tf_op jit(solution)/shard_map/ppermute | solution.py:163
  24.1 14.0 %collective-permute-start.3 = (f32[128,256]{0,1:T(8,128)S(1)}, f32[128,256]{0,1:T(8,128)S(1)}, u32[]{:S(2)}, u32[]{:S(2)}) collective-permute-start(f32[128,256]{0,1:T(8,128)S(1)} %get-tuple-element.137), channel_id=1, source_target_pairs={{0,12},{1,0},{2,4},{3,8},{4,28},{5,16},{6,20},{7,24},{8,13},{9,1},... | collective-permute-start | bytes 393224 | tf_op jit(solution)/shard_map/ppermute | solution.py:163
  27.2 10.9 %collective-permute-start.2 = (f32[128,256]{0,1:T(8,128)S(1)}, f32[128,256]{0,1:T(8,128)S(1)}, u32[]{:S(2)}, u32[]{:S(2)}) collective-permute-start(f32[128,256]{0,1:T(8,128)S(1)} %get-tuple-element.138), channel_id=1, source_target_pairs={{0,8},{1,12},{2,0},{3,4},{4,24},{5,28},{6,16},{7,20},{8,9},{9,13},... | collective-permute-start | bytes 393224 | tf_op jit(solution)/shard_map/ppermute | solution.py:163
  29.5 8.6 %collective-permute-start = (f32[128,256]{0,1:T(8,128)S(1)}, f32[128,256]{0,1:T(8,128)S(1)}, u32[]{:S(2)}, u32[]{:S(2)}) collective-permute-start(f32[128,256]{0,1:T(8,128)S(1)} %get-tuple-element.139), channel_id=1, source_target_pairs={{0,0},{1,4},{2,8},{3,12},{4,16},{5,20},{6,24},{7,28},{8,1},{9,5},{... | collective-permute-start | bytes 393224 | tf_op jit(solution)/shard_map/ppermute | solution.py:163
  38.2 16.4 %collective-permute-start.7 = (f32[128,256]{0,1:T(8,128)S(1)}, f32[128,256]{0,1:T(8,128)S(1)}, u32[]{:S(2)}, u32[]{:S(2)}) collective-permute-start(f32[128,256]{0,1:T(8,128)S(1)} %add_add_fusion.2), channel_id=1, source_target_pairs={{24,0},{28,4},{0,8},{4,12},{8,16},{12,20},{16,24},{20,28},{25,1},{... | collective-permute-start | bytes 393224 | tf_op jit(solution)/shard_map/ppermute | solution.py:142
  39.7 14.9 %collective-permute-start.6 = (f32[128,256]{0,1:T(8,128)S(1)}, f32[128,256]{0,1:T(8,128)S(1)}, u32[]{:S(2)}, u32[]{:S(2)}) collective-permute-start(f32[128,256]{0,1:T(8,128)S(1)} %add_add_fusion.2), channel_id=1, source_target_pairs={{16,0},{20,4},{24,8},{28,12},{0,16},{4,20},{8,24},{12,28},{17,1},{... | collective-permute-start | bytes 393224 | tf_op jit(solution)/shard_map/ppermute | solution.py:142
  40.3 14.4 %collective-permute-start.5 = (f32[128,256]{0,1:T(8,128)S(1)}, f32[128,256]{0,1:T(8,128)S(1)}, u32[]{:S(2)}, u32[]{:S(2)}) collective-permute-start(f32[128,256]{0,1:T(8,128)S(1)} %add_add_fusion.2), channel_id=1, source_target_pairs={{8,0},{12,4},{16,8},{20,12},{24,16},{28,20},{0,24},{4,28},{9,1},{1... | collective-permute-start | bytes 393224 | tf_op jit(solution)/shard_map/ppermute | solution.py:142
  54.6 3.8 %copy-start.29 = (f32[2,512,128]{2,1,0:T(8,128)S(1)}, f32[2,512,128]{2,1,0:T(8,128)}, u32[]{:S(2)}) copy-start(f32[2,512,128]{2,1,0:T(8,128)} %param.16) | copy-start | bytes 1572868
  54.8 9.5 %collective-permute-start.8 = (f32[4,128,256]{1,2,0:T(8,128)S(1)}, f32[4,128,256]{1,2,0:T(8,128)}, u32[]{:S(2)}, u32[]{:S(2)}) collective-permute-start(f32[4,128,256]{1,2,0:T(8,128)S(1)} %constant_dynamic-slice_fusion.8), channel_id=1, source_target_pairs={{0,4},{4,0},{8,12},{12,8},{16,20},{20,16},{24,28},{28,24},{1,5},{5... | collective-permute-start | bytes 1572872 | tf_op jit(solution)/shard_map/ppermute | solution.py:145
  56.0 6.8 %collective-permute-start.14 = (f32[8,2,1024]{2,0,1:T(8,128)}, f32[8,2,1024]{2,0,1:T(8,128)}, u32[]{:S(2)}, u32[]{:S(2)}) collective-permute-start(f32[8,2,1024]{2,0,1:T(8,128)} %stack.156), channel_id=1, source_target_pairs={{3,0},{0,1},{1,2},{2,3},{7,4},{4,5},{5,6},{6,7},{11,8},{8,9},{9,10... | collective-permute-start | bytes 196616 | tf_op jit(solution)/shard_map/ppermute | solution.py:138
  58.4 3.5 %collective-permute-start.13 = (f32[8,2,1024]{2,0,1:T(8,128)}, f32[8,2,1024]{2,0,1:T(8,128)}, u32[]{:S(2)}, u32[]{:S(2)}) collective-permute-start(f32[8,2,1024]{2,0,1:T(8,128)} %stack.156), channel_id=1, source_target_pairs={{2,0},{3,1},{0,2},{1,3},{6,4},{7,5},{4,6},{5,7},{10,8},{11,9},{8,1... | collective-permute-start | bytes 196616 | tf_op jit(solution)/shard_map/ppermute | solution.py:138
  65.8 41.5 %copy-start.19 = (f32[4,2,128,256]{3,2,1,0:T(8,128)}, f32[4,2,128,256]{3,2,1,0:T(8,128)S(1)}, u32[]{:S(2)}) copy-start(f32[4,2,128,256]{3,2,1,0:T(8,128)S(1)} %copy.69) | copy-start | bytes 3145732
  65.8 4.1 %copy-start.22 = (f32[2,512,1024]{2,1,0:T(8,128)S(1)}, f32[2,512,1024]{2,1,0:T(8,128)}, u32[]{:S(2)}) copy-start(f32[2,512,1024]{2,1,0:T(8,128)} %param.14) | copy-start | bytes 12582916
  69.9 14.5 %copy-start.31 = (f32[8,2,2048]{2,0,1:T(8,128)S(1)}, f32[8,2,2048]{2,0,1:T(8,128)}, u32[]{:S(2)}) copy-start(f32[8,2,2048]{2,0,1:T(8,128)} %copy-done.30) | copy-start | bytes 393220
  72.0 13.1 %collective-permute-start.10 = (f32[128,256]{0,1:T(8,128)S(1)}, f32[128,256]{0,1:T(8,128)S(1)}, u32[]{:S(2)}, u32[]{:S(2)}) collective-permute-start(f32[128,256]{0,1:T(8,128)S(1)} %get-tuple-element.130), channel_id=1, source_target_pairs={{0,4},{1,8},{2,12},{3,0},{4,20},{5,24},{6,28},{7,16},{8,5},{9,9},{... | collective-permute-start | bytes 393224 | tf_op jit(solution)/shard_map/ppermute | solution.py:163
  75.6 9.4 %collective-permute-start.12 = (f32[128,256]{0,1:T(8,128)S(1)}, f32[128,256]{0,1:T(8,128)S(1)}, u32[]{:S(2)}, u32[]{:S(2)}) collective-permute-start(f32[128,256]{0,1:T(8,128)S(1)} %get-tuple-element.131), channel_id=1, source_target_pairs={{0,12},{1,0},{2,4},{3,8},{4,28},{5,16},{6,20},{7,24},{8,13},{9,1},... | collective-permute-start | bytes 393224 | tf_op jit(solution)/shard_map/ppermute | solution.py:163
  79.0 6.1 %collective-permute-start.11 = (f32[128,256]{0,1:T(8,128)S(1)}, f32[128,256]{0,1:T(8,128)S(1)}, u32[]{:S(2)}, u32[]{:S(2)}) collective-permute-start(f32[128,256]{0,1:T(8,128)S(1)} %get-tuple-element.132), channel_id=1, source_target_pairs={{0,8},{1,12},{2,0},{3,4},{4,24},{5,28},{6,16},{7,20},{8,9},{9,13},... | collective-permute-start | bytes 393224 | tf_op jit(solution)/shard_map/ppermute | solution.py:163
  82.5 6.8 %collective-permute-start.9 = (f32[128,256]{0,1:T(8,128)S(1)}, f32[128,256]{0,1:T(8,128)S(1)}, u32[]{:S(2)}, u32[]{:S(2)}) collective-permute-start(f32[128,256]{0,1:T(8,128)S(1)} %get-tuple-element.133), channel_id=1, source_target_pairs={{0,0},{1,4},{2,8},{3,12},{4,16},{5,20},{6,24},{7,28},{8,1},{9,5},{... | collective-permute-start | bytes 393224 | tf_op jit(solution)/shard_map/ppermute | solution.py:163
  89.4 17.6 %collective-permute-start.17 = (f32[128,256]{0,1:T(8,128)S(1)}, f32[128,256]{0,1:T(8,128)S(1)}, u32[]{:S(2)}, u32[]{:S(2)}) collective-permute-start(f32[128,256]{0,1:T(8,128)S(1)} %add_add_fusion.1), channel_id=1, source_target_pairs={{24,0},{28,4},{0,8},{4,12},{8,16},{12,20},{16,24},{20,28},{25,1},{... | collective-permute-start | bytes 393224 | tf_op jit(solution)/shard_map/ppermute | solution.py:142
  92.7 14.3 %collective-permute-start.16 = (f32[128,256]{0,1:T(8,128)S(1)}, f32[128,256]{0,1:T(8,128)S(1)}, u32[]{:S(2)}, u32[]{:S(2)}) collective-permute-start(f32[128,256]{0,1:T(8,128)S(1)} %add_add_fusion.1), channel_id=1, source_target_pairs={{16,0},{20,4},{24,8},{28,12},{0,16},{4,20},{8,24},{12,28},{17,1},{... | collective-permute-start | bytes 393224 | tf_op jit(solution)/shard_map/ppermute | solution.py:142
  93.3 13.7 %collective-permute-start.15 = (f32[128,256]{0,1:T(8,128)S(1)}, f32[128,256]{0,1:T(8,128)S(1)}, u32[]{:S(2)}, u32[]{:S(2)}) collective-permute-start(f32[128,256]{0,1:T(8,128)S(1)} %add_add_fusion.1), channel_id=1, source_target_pairs={{8,0},{12,4},{16,8},{20,12},{24,16},{28,20},{0,24},{4,28},{9,1},{1... | collective-permute-start | bytes 393224 | tf_op jit(solution)/shard_map/ppermute | solution.py:142
  107.2 4.3 %collective-permute-start.18 = (f32[4,128,256]{1,2,0:T(8,128)S(1)}, f32[4,128,256]{1,2,0:T(8,128)}, u32[]{:S(2)}, u32[]{:S(2)}) collective-permute-start(f32[4,128,256]{1,2,0:T(8,128)S(1)} %constant_dynamic-slice_fusion.3), channel_id=1, source_target_pairs={{0,4},{4,0},{8,12},{12,8},{16,20},{20,16},{24,28},{28,24},{1,5},{5... | collective-permute-start | bytes 1572872 | tf_op jit(solution)/shard_map/ppermute | solution.py:145
  107.3 18.4 %collective-permute-start.33 = (f32[512,256]{1,0:T(8,128)S(1)}, f32[512,256]{1,0:T(8,128)}, u32[]{:S(2)}, u32[]{:S(2)}) collective-permute-start(f32[512,256]{1,0:T(8,128)S(1)} %constant_dynamic-slice_fusion), channel_id=1, source_target_pairs={{3,0},{0,1},{1,2},{2,3},{7,4},{4,5},{5,6},{6,7},{11,8},{8,9},{9,10... | collective-permute-start | bytes 1572872 | tf_op jit(solution)/shard_map/ppermute | solution.py:138
  109.6 26.1 %collective-permute-start.32 = (f32[512,256]{1,0:T(8,128)S(1)}, f32[512,256]{1,0:T(8,128)}, u32[]{:S(2)}, u32[]{:S(2)}) collective-permute-start(f32[512,256]{1,0:T(8,128)S(1)} %constant_dynamic-slice_fusion), channel_id=1, source_target_pairs={{2,0},{3,1},{0,2},{1,3},{6,4},{7,5},{4,6},{5,7},{10,8},{11,9},{8,1... | collective-permute-start | bytes 1572872 | tf_op jit(solution)/shard_map/ppermute | solution.py:138
  110.7 32.9 %collective-permute-start.31 = (f32[512,256]{1,0:T(8,128)S(1)}, f32[512,256]{1,0:T(8,128)}, u32[]{:S(2)}, u32[]{:S(2)}) collective-permute-start(f32[512,256]{1,0:T(8,128)S(1)} %constant_dynamic-slice_fusion), channel_id=1, source_target_pairs={{1,0},{2,1},{3,2},{0,3},{5,4},{6,5},{7,6},{4,7},{9,8},{10,9},{11,1... | collective-permute-start | bytes 1572872 | tf_op jit(solution)/shard_map/ppermute | solution.py:138
  113.0 3.8 %copy-start.23 = (f32[2,512,1024]{2,1,0:T(8,128)S(1)}, f32[2,512,1024]{2,1,0:T(8,128)}, u32[]{:S(2)}) copy-start(f32[2,512,1024]{2,1,0:T(8,128)} %param.13) | copy-start | bytes 12582916
  116.8 34.6 %copy-start.5 = (f32[8,2048]{1,0:T(8,128)S(1)}, f32[8,2048]{1,0:T(8,128)}, u32[]{:S(2)}) copy-start(f32[8,2048]{1,0:T(8,128)} %get-tuple-element.67.sources_ref) | copy-start | bytes 196612
  118.9 24.7 %collective-permute-start.20 = (f32[128,256]{0,1:T(8,128)S(1)}, f32[128,256]{0,1:T(8,128)S(1)}, u32[]{:S(2)}, u32[]{:S(2)}) collective-permute-start(f32[128,256]{0,1:T(8,128)S(1)} %get-tuple-element.126), channel_id=1, source_target_pairs={{0,4},{1,8},{2,12},{3,0},{4,20},{5,24},{6,28},{7,16},{8,5},{9,9},{... | collective-permute-start | bytes 393224 | tf_op jit(solution)/shard_map/ppermute | solution.py:163
  122.6 21.0 %collective-permute-start.22 = (f32[128,256]{0,1:T(8,128)S(1)}, f32[128,256]{0,1:T(8,128)S(1)}, u32[]{:S(2)}, u32[]{:S(2)}) collective-permute-start(f32[128,256]{0,1:T(8,128)S(1)} %get-tuple-element.127), channel_id=1, source_target_pairs={{0,12},{1,0},{2,4},{3,8},{4,28},{5,16},{6,20},{7,24},{8,13},{9,1},... | collective-permute-start | bytes 393224 | tf_op jit(solution)/shard_map/ppermute | solution.py:163
  125.7 17.9 %collective-permute-start.21 = (f32[128,256]{0,1:T(8,128)S(1)}, f32[128,256]{0,1:T(8,128)S(1)}, u32[]{:S(2)}, u32[]{:S(2)}) collective-permute-start(f32[128,256]{0,1:T(8,128)S(1)} %get-tuple-element.128), channel_id=1, source_target_pairs={{0,8},{1,12},{2,0},{3,4},{4,24},{5,28},{6,16},{7,20},{8,9},{9,13},... | collective-permute-start | bytes 393224 | tf_op jit(solution)/shard_map/ppermute | solution.py:163
  135.7 9.8 %collective-permute-start.19 = (f32[128,256]{0,1:T(8,128)S(1)}, f32[128,256]{0,1:T(8,128)S(1)}, u32[]{:S(2)}, u32[]{:S(2)}) collective-permute-start(f32[128,256]{0,1:T(8,128)S(1)} %get-tuple-element.129), channel_id=1, source_target_pairs={{0,0},{1,4},{2,8},{3,12},{4,16},{5,20},{6,24},{7,28},{8,1},{9,5},{... | collective-permute-start | bytes 393224 | tf_op jit(solution)/shard_map/ppermute | solution.py:163
  145.5 14.6 %collective-permute-start.25 = (f32[128,256]{0,1:T(8,128)S(1)}, f32[128,256]{0,1:T(8,128)S(1)}, u32[]{:S(2)}, u32[]{:S(2)}) collective-permute-start(f32[128,256]{0,1:T(8,128)S(1)} %add_add_fusion), channel_id=1, source_target_pairs={{24,0},{28,4},{0,8},{4,12},{8,16},{12,20},{16,24},{20,28},{25,1},{... | collective-permute-start | bytes 393224 | tf_op jit(solution)/shard_map/ppermute | solution.py:142
  148.7 11.5 %collective-permute-start.24 = (f32[128,256]{0,1:T(8,128)S(1)}, f32[128,256]{0,1:T(8,128)S(1)}, u32[]{:S(2)}, u32[]{:S(2)}) collective-permute-start(f32[128,256]{0,1:T(8,128)S(1)} %add_add_fusion), channel_id=1, source_target_pairs={{16,0},{20,4},{24,8},{28,12},{0,16},{4,20},{8,24},{12,28},{17,1},{... | collective-permute-start | bytes 393224 | tf_op jit(solution)/shard_map/ppermute | solution.py:142
  149.7 10.5 %collective-permute-start.23 = (f32[128,256]{0,1:T(8,128)S(1)}, f32[128,256]{0,1:T(8,128)S(1)}, u32[]{:S(2)}, u32[]{:S(2)}) collective-permute-start(f32[128,256]{0,1:T(8,128)S(1)} %add_add_fusion), channel_id=1, source_target_pairs={{8,0},{12,4},{16,8},{20,12},{24,16},{28,20},{0,24},{4,28},{9,1},{1... | collective-permute-start | bytes 393224 | tf_op jit(solution)/shard_map/ppermute | solution.py:142
  160.1 3.8 %copy-start.13 = (bf16[768,2048]{1,0:T(8,128)(2,1)}, bf16[768,2048]{1,0:T(8,128)(2,1)S(1)}, u32[]{:S(2)}) copy-start(bf16[768,2048]{1,0:T(8,128)(2,1)S(1)} %get-tuple-element.98) | copy-start | bytes 9437188
  160.4 4.3 %collective-permute-start.26 = (f32[4,128,256]{1,2,0:T(8,128)S(1)}, f32[4,128,256]{1,2,0:T(8,128)S(1)}, u32[]{:S(2)}, u32[]{:S(2)}) collective-permute-start(f32[4,128,256]{1,2,0:T(8,128)S(1)} %constant_dynamic-slice_fusion.2), channel_id=1, source_target_pairs={{0,4},{4,0},{8,12},{12,8},{16,20},{20,16},{24,28},{28,24},{1,5},{5... | collective-permute-start | bytes 1572872 | tf_op jit(solution)/shard_map/ppermute | solution.py:145
  163.9 18.7 %collective-permute-start.34 = (f32[3,512,256]{2,1,0:T(8,128)}, f32[3,512,256]{2,1,0:T(8,128)}, u32[]{:S(2)}, u32[]{:S(2)}) collective-permute-start(f32[3,512,256]{2,1,0:T(8,128)} %pad_maximum_fusion.5), channel_id=1, source_target_pairs={{0,4},{4,0},{8,12},{12,8},{16,20},{20,16},{24,28},{28,24},{1,5},{5... | collective-permute-start | bytes 4718600 | tf_op jit(solution)/shard_map/ppermute | solution.py:145
  169.5 18.4 %collective-permute-start.29 = (f32[512,256]{1,0:T(8,128)S(1)}, f32[512,256]{1,0:T(8,128)S(1)}, u32[]{:S(2)}, u32[]{:S(2)}) collective-permute-start(f32[512,256]{1,0:T(8,128)S(1)} %constant_dynamic-slice_fusion.1), channel_id=1, source_target_pairs={{3,0},{0,1},{1,2},{2,3},{7,4},{4,5},{5,6},{6,7},{11,8},{8,9},{9,10... | collective-permute-start | bytes 1572872 | tf_op jit(solution)/shard_map/ppermute | solution.py:138
  169.5 24.6 %collective-permute-start.28 = (f32[512,256]{1,0:T(8,128)S(1)}, f32[512,256]{1,0:T(8,128)S(1)}, u32[]{:S(2)}, u32[]{:S(2)}) collective-permute-start(f32[512,256]{1,0:T(8,128)S(1)} %constant_dynamic-slice_fusion.1), channel_id=1, source_target_pairs={{2,0},{3,1},{0,2},{1,3},{6,4},{7,5},{4,6},{5,7},{10,8},{11,9},{8,1... | collective-permute-start | bytes 1572872 | tf_op jit(solution)/shard_map/ppermute | solution.py:138
  170.7 24.5 %collective-permute-start.27 = (f32[512,256]{1,0:T(8,128)S(1)}, f32[512,256]{1,0:T(8,128)S(1)}, u32[]{:S(2)}, u32[]{:S(2)}) collective-permute-start(f32[512,256]{1,0:T(8,128)S(1)} %constant_dynamic-slice_fusion.1), channel_id=1, source_target_pairs={{1,0},{2,1},{3,2},{0,3},{5,4},{6,5},{7,6},{4,7},{9,8},{10,9},{11,1... | collective-permute-start | bytes 1572872 | tf_op jit(solution)/shard_map/ppermute | solution.py:138
  182.5 4.5 %copy-start.15 = (bf16[768,2048]{1,0:T(8,128)(2,1)}, bf16[768,2048]{1,0:T(8,128)(2,1)S(1)}, u32[]{:S(2)}) copy-start(bf16[768,2048]{1,0:T(8,128)(2,1)S(1)} %get-tuple-element.100) | copy-start | bytes 9437188
  182.5 4.5 %copy-start.17 = (bf16[768,2048]{1,0:T(8,128)(2,1)}, bf16[768,2048]{1,0:T(8,128)(2,1)S(1)}, u32[]{:S(2)}) copy-start(bf16[768,2048]{1,0:T(8,128)(2,1)S(1)} %get-tuple-element.101) | copy-start | bytes 9437188
  187.8 8.3 %copy-start.20 = (f32[4,2,128,256]{3,2,1,0:T(8,128)S(1)}, f32[4,2,128,256]{3,2,1,0:T(8,128)}, u32[]{:S(2)}) copy-start(f32[4,2,128,256]{3,2,1,0:T(8,128)} %copy-done.19) | copy-start | bytes 3145732
  195.3 9.4 %collective-permute-start.30 = (f32[3,512,256]{2,1,0:T(8,128)S(1)}, f32[3,512,256]{2,1,0:T(8,128)S(1)}, u32[]{:S(2)}, u32[]{:S(2)}) collective-permute-start(f32[3,512,256]{2,1,0:T(8,128)S(1)} %pad_maximum_fusion.4), channel_id=1, source_target_pairs={{0,4},{4,0},{8,12},{12,8},{16,20},{20,16},{24,28},{28,24},{1,5},{5... | collective-permute-start | bytes 4718600 | tf_op jit(solution)/shard_map/ppermute | solution.py:145
  197.1 5.6 %copy-start.3 = (bf16[4096,256]{1,0:T(8,128)(2,1)}, bf16[4096,256]{1,0:T(8,128)(2,1)S(1)}, u32[]{:S(2)}) copy-start(bf16[4096,256]{1,0:T(8,128)(2,1)S(1)} %get-tuple-element.90) | copy-start | bytes 6291460
  197.1 3.7 %copy-start.12 = (bf16[768,2048]{1,0:T(8,128)(2,1)S(1)}, bf16[768,2048]{1,0:T(8,128)(2,1)}, u32[]{:S(2)}) copy-start(bf16[768,2048]{1,0:T(8,128)(2,1)} %copy-done.11) | copy-start | bytes 9437188
  227.4 3.1 %copy-start.28 = (f32[768,256]{0,1:T(8,128)S(1)}, f32[768,256]{0,1:T(8,128)}, u32[]{:S(2)}) copy-start(f32[768,256]{0,1:T(8,128)} %fusion.57) | copy-start | bytes 2359300
  (19 other events, 36.6 us)

commit v3 on v2

--- a/solution.py
+++ b/solution.py
@@ -239,8 +239,8 @@
     bottom_solved, source_part = lax.optimization_barrier((bottom_solved, sources_of(1, 1)))
     tiles[1][1] = green_tiles(points, source_part)
     bottom_full = whole(bottom_solved)
-    top_solved, bottom_solved, bottom_full, tiles[1][1] = lax.optimization_barrier(
-        (top_solved, bottom_solved, bottom_full, tiles[1][1])
+    top_solved, bottom_solved, tiles[1][1] = lax.optimization_barrier(
+        (top_solved, bottom_solved, tiles[1][1])
     )
 
     elevation = term(0, top_full) + term(1, bottom_full)

time: 236 us -> 218 us (0.924)
  waiting for transfers between devices: 23.4 us -> 7.74 us
  starting transfers between devices: 77.9 us -> 84.9 us
  other arithmetic: 24.1 us -> 17.6 us
  matrix products: 29.8 us -> 26.8 us
    ppermute x5, starting transfers between devices: 3.84 us -> 19.6 us  [sibling(): return lax.ppermute(piece, 'row', [(i, i ^ 1) for i in range(row_size)])]
    ppermute x9, waiting for transfers between devices: 17.2 us -> 2.45 us  [shift_col(): return lax.ppermute(piece, 'col', pairs)]
    ppermute x9, starting transfers between devices: 15.7 us -> 9.46 us  [shift_chip(): return lax.ppermute(piece, 'row', pairs)]
    another operation x10, other arithmetic: 9.12 us -> 4.78 us  [by_core(): return jnp.stack([first, second], axis=axis)]
    ppermute x12, waiting for transfers between devices: 6.14 us -> 3.72 us  [columns(): total = total + lax.ppermute(piece, ('row', 'col'), pairs)]
    unnamed x89 -> x81, local copies, waits for them, and re-layouts: 19.4 us -> 20.6 us
  transfers between devices with their start and end apart: 35 -> 35, of which waited for: 6 -> 5; matrix products, arithmetic and copies ran while one was open for 18% -> 16% of each run, Pallas kernels for 15% -> 16%
where the time goes in v3:
time: 218 us; the launch traced here: 216 us
  starting transfers between devices  84.9 us (39%)
  local copies, waits for them, and re-layouts  40.3 us (18%)
  Pallas kernels  36.5 us (17%)
  matrix products  26.8 us (12%)
  other arithmetic  17.6 us (8%)
  waiting for transfers between devices  7.74 us (4%)
  between operations  2.48 us (1%)
    ppermute x12, starting transfers between devices, columns(): total = total + lax.ppermute(piece, ('row', 'col'), pairs)  43.6 us
    pallas_call x4, Pallas kernels, green_tiles(): pl.pallas_call(green_kernel, grid=(point_count // tile,), in_specs=[pl.Bl...  34.8 us
    unnamed x81, local copies, waits for them, and re-layouts  20.6 us
    ppermute x5, starting transfers between devices, sibling(): return lax.ppermute(piece, 'row', [(i, i ^ 1) for i in range(row_size)])  19.6 us
    dot_general x6, matrix products, product(): return dot(matrix[0], vector) + dot(matrix[1], turned(vector))  18.5 us
    ppermute x9, starting transfers between devices, shift_col(): return lax.ppermute(piece, 'col', pairs)  12.2 us
    ppermute x9, starting transfers between devices, shift_chip(): return lax.ppermute(piece, 'row', pairs)  9.46 us
    another operation x4, local copies, waits for them, and re-layouts, per_device(): jnp.stack([top_solved, bottom_solved]).reshape(2, col_rows, 2, right_count)  9 us
  transfers between devices with their start and end apart: 35, of which 5 were waited for; matrix products, arithmetic and copies ran while one was open for 16% of the time, Pallas kernels for 16%

profile of v3, /device:TPU:1, one launch (start us, length us, event | category | flops | bytes accessed | tf_op | source)
XLA Modules:
  0.0 216.3 jit_solution(7371001810932887739)
XLA Ops:
  3.1 3.4 %fusion.8 = f32[256,512]{1,0:T(8,128)S(1)} fusion(f32[2,512,1024]{2,1,0:T(8,128)} %param.12, f32[1024,128]{1,0:T(8,128)S(1)} %get-tuple-element.123, f32[1024,128]{1,0:T(8,128)S(1)} %fusion.69), kind=kOutput, calls=%fused_computation.13 | convolution fusion | flops 805568512 | bytes 3670016 | tf_op jit(solution)/shard_map/dot_general | solution.py:128
  6.6 3.5 %fusion.22 = f32[256,512]{1,0:T(8,128)S(1)} fusion(f32[256,512]{1,0:T(8,128)S(1)} %fusion.8, f32[2,512,1024]{2,1,0:T(8,128)} %param.12, f32[1024,128]{1,0:T(8,128)S(1)} %get-tuple-element.122, f32[1024,128]{1,0:T(8,128)S(1)} %get-tuple-element.123), kind=kOutput, calls=%fused_computation.36 | convolution fusion | flops 805699584 | bytes 4194304 | tf_op jit(solution)/shard_map/dot_general | solution.py:128
  10.1 5.6 %collective-permute-start = (f32[128,256]{0,1:T(8,128)S(1)}, f32[128,256]{0,1:T(8,128)S(1)}, u32[]{:S(2)}, u32[]{:S(2)}) collective-permute-start(f32[128,256]{0,1:T(8,128)S(1)} %get-tuple-element.137), channel_id=1, source_target_pairs={{0,0},{1,4},{2,8},{3,12},{4,16},{5,20},{6,24},{7,28},{8,1},{9,5},{... | collective-permute-start | bytes 393224 | tf_op jit(solution)/shard_map/ppermute | solution.py:163
  15.7 3.1 %collective-permute-start.1 = (f32[128,256]{0,1:T(8,128)S(1)}, f32[128,256]{0,1:T(8,128)S(1)}, u32[]{:S(2)}, u32[]{:S(2)}) collective-permute-start(f32[128,256]{0,1:T(8,128)S(1)} %get-tuple-element.134), channel_id=1, source_target_pairs={{0,4},{1,8},{2,12},{3,0},{4,20},{5,24},{6,28},{7,16},{8,5},{9,9},{... | collective-permute-start | bytes 393224 | tf_op jit(solution)/shard_map/ppermute | solution.py:163
  18.9 4.6 %collective-permute-start.2 = (f32[128,256]{0,1:T(8,128)S(1)}, f32[128,256]{0,1:T(8,128)S(1)}, u32[]{:S(2)}, u32[]{:S(2)}) collective-permute-start(f32[128,256]{0,1:T(8,128)S(1)} %get-tuple-element.136), channel_id=1, source_target_pairs={{0,8},{1,12},{2,0},{3,4},{4,24},{5,28},{6,16},{7,20},{8,9},{9,13},... | collective-permute-start | bytes 393224 | tf_op jit(solution)/shard_map/ppermute | solution.py:163
  23.5 1.9 collective-permute-start.3
  26.8 2.5 %select_multiply_fusion = (f32[2,1024]{1,0:T(2,128)S(1)}, f32[1,2,1024]{2,1,0:T(2,128)S(1)}, f32[1,2,1024]{2,1,0:T(2,128)S(1)}) fusion(f32[]{:T(128)} %bitcast.14, f32[]{:T(128)} %bitcast.13, f32[2,1024]{1,0:T(2,128)S(1)} %copy-done.25, f32[]{:T(128)} %bitcast.155, f32[]{:T(128)S(6)} %mul.83, s32[2,1024]{1,0:T(2,128)S(1)} %copy-done.26, f32[]{:T(128)} %bitcast.11, ...), kind=kLoop, calls=%fused_computation.126 | loop fusion | flops 18432 | bytes 40984 | tf_op jit(solution)/shard_map/mul | solution.py:190
  30.1 2.1 collective-permute-start.4
  37.1 8.7 %shard_map.131 = (bf16[768,2048]{1,0:T(8,128)(2,1)S(1)}, bf16[768,2048]{1,0:T(8,128)(2,1)S(1)}) custom-call(f32[768,8]{1,0:T(8,128)S(1)} %bitcast.156, f32[8,2048]{1,0:T(8,128)S(1)} %get-tuple-element.52.sources_ref), custom_call_target="tpu_custom_call" | custom-call | flops 6291456000 | bytes 6291456 | tf_op jit(solution)/shard_map/pallas_call | solution.py:61
  47.4 1.7 copy-done.4
  49.3 2.3 %collective-permute-start.8 = (f32[4,128,256]{1,2,0:T(8,128)S(1)}, f32[4,128,256]{1,2,0:T(8,128)S(1)}, u32[]{:S(2)}, u32[]{:S(2)}) collective-permute-start(f32[4,128,256]{1,2,0:T(8,128)S(1)} %constant_dynamic-slice_fusion.8), channel_id=1, source_target_pairs={{0,4},{4,0},{8,12},{12,8},{16,20},{20,16},{24,28},{28,24},{1,5},{5... | collective-permute-start | bytes 1572872 | tf_op jit(solution)/shard_map/ppermute | solution.py:145
  51.7 1.8 collective-permute-start.13
  54.5 1.6 collective-permute-done.13
  59.8 4.0 %fusion.4 = f32[256,512]{1,0:T(8,128)S(1)} fusion(f32[2,512,1024]{2,1,0:T(8,128)} %param.14, f32[1024,128]{1,0:T(8,128)S(1)} %get-tuple-element.119, f32[1024,128]{1,0:T(8,128)S(1)} %get-tuple-element.118), kind=kOutput, calls=%fused_computation.9 | convolution fusion | flops 805568512 | bytes 3670016 | tf_op jit(solution)/shard_map/dot_general | solution.py:128
  63.9 2.0 fusion.31
  65.9 3.4 %collective-permute-start.10 = (f32[128,256]{0,1:T(8,128)S(1)}, f32[128,256]{0,1:T(8,128)S(1)}, u32[]{:S(2)}, u32[]{:S(2)}) collective-permute-start(f32[128,256]{0,1:T(8,128)S(1)} %get-tuple-element.128), channel_id=1, source_target_pairs={{0,4},{1,8},{2,12},{3,0},{4,20},{5,24},{6,28},{7,16},{8,5},{9,9},{... | collective-permute-start | bytes 393224 | tf_op jit(solution)/shard_map/ppermute | solution.py:163
  69.4 2.7 %collective-permute-start.11 = (f32[128,256]{0,1:T(8,128)S(1)}, f32[128,256]{0,1:T(8,128)S(1)}, u32[]{:S(2)}, u32[]{:S(2)}) collective-permute-start(f32[128,256]{0,1:T(8,128)S(1)} %get-tuple-element.130), channel_id=1, source_target_pairs={{0,8},{1,12},{2,0},{3,4},{4,24},{5,28},{6,16},{7,20},{8,9},{9,13},... | collective-permute-start | bytes 393224 | tf_op jit(solution)/shard_map/ppermute | solution.py:163
  72.1 2.9 %collective-permute-start.12 = (f32[128,256]{0,1:T(8,128)S(1)}, f32[128,256]{0,1:T(8,128)S(1)}, u32[]{:S(2)}, u32[]{:S(2)}) collective-permute-start(f32[128,256]{0,1:T(8,128)S(1)} %get-tuple-element.129), channel_id=1, source_target_pairs={{0,12},{1,0},{2,4},{3,8},{4,28},{5,16},{6,20},{7,24},{8,13},{9,1},... | collective-permute-start | bytes 393224 | tf_op jit(solution)/shard_map/ppermute | solution.py:163
  75.0 5.0 %collective-permute-start.9 = (f32[128,256]{0,1:T(8,128)S(1)}, f32[128,256]{0,1:T(8,128)S(1)}, u32[]{:S(2)}, u32[]{:S(2)}) collective-permute-start(f32[128,256]{0,1:T(8,128)S(1)} %get-tuple-element.131), channel_id=1, source_target_pairs={{0,0},{1,4},{2,8},{3,12},{4,16},{5,20},{6,24},{7,28},{8,1},{9,5},{... | collective-permute-start | bytes 393224 | tf_op jit(solution)/shard_map/ppermute | solution.py:163
  82.0 4.9 %collective-permute-start.15 = (f32[128,256]{0,1:T(8,128)S(1)}, f32[128,256]{0,1:T(8,128)S(1)}, u32[]{:S(2)}, u32[]{:S(2)}) collective-permute-start(f32[128,256]{0,1:T(8,128)S(1)} %add_add_fusion.1), channel_id=1, source_target_pairs={{8,0},{12,4},{16,8},{20,12},{24,16},{28,20},{0,24},{4,28},{9,1},{1... | collective-permute-start | bytes 393224 | tf_op jit(solution)/shard_map/ppermute | solution.py:142
  87.3 8.7 %shard_map.132 = (bf16[768,2048]{1,0:T(8,128)(2,1)S(1)}, bf16[768,2048]{1,0:T(8,128)(2,1)S(1)}) custom-call(f32[768,8]{1,0:T(8,128)S(1)} %bitcast.157, f32[8,2048]{1,0:T(8,128)S(1)} %get-tuple-element.59.sources_ref), custom_call_target="tpu_custom_call" | custom-call | flops 6291456000 | bytes 6291456 | tf_op jit(solution)/shard_map/pallas_call | solution.py:61
  96.0 1.8 copy-done.6
  97.8 1.6 copy-done.8
  99.7 1.9 collective-permute-start.18
  103.7 3.7 %fusion = f32[256,512]{1,0:T(8,128)S(1)} fusion(f32[2,512,1024]{2,1,0:T(8,128)} %param.13, f32[1024,128]{1,0:T(8,128)S(1)} %get-tuple-element.115, f32[1024,128]{1,0:T(8,128)S(1)} %get-tuple-element.114), kind=kOutput, calls=%fused_computation.5 | convolution fusion | flops 805568512 | bytes 3670016 | tf_op jit(solution)/shard_map/dot_general | solution.py:128
  107.5 1.9 fusion.34
  109.5 4.2 %collective-permute-start.19 = (f32[128,256]{0,1:T(8,128)S(1)}, f32[128,256]{0,1:T(8,128)S(1)}, u32[]{:S(2)}, u32[]{:S(2)}) collective-permute-start(f32[128,256]{0,1:T(8,128)S(1)} %get-tuple-element.127), channel_id=1, source_target_pairs={{0,0},{1,4},{2,8},{3,12},{4,16},{5,20},{6,24},{7,28},{8,1},{9,5},{... | collective-permute-start | bytes 393224 | tf_op jit(solution)/shard_map/ppermute | solution.py:163
  113.7 3.5 %collective-permute-start.20 = (f32[128,256]{0,1:T(8,128)S(1)}, f32[128,256]{0,1:T(8,128)S(1)}, u32[]{:S(2)}, u32[]{:S(2)}) collective-permute-start(f32[128,256]{0,1:T(8,128)S(1)} %get-tuple-element.124), channel_id=1, source_target_pairs={{0,4},{1,8},{2,12},{3,0},{4,20},{5,24},{6,28},{7,16},{8,5},{9,9},{... | collective-permute-start | bytes 393224 | tf_op jit(solution)/shard_map/ppermute | solution.py:163
  117.1 4.5 %collective-permute-start.21 = (f32[128,256]{0,1:T(8,128)S(1)}, f32[128,256]{0,1:T(8,128)S(1)}, u32[]{:S(2)}, u32[]{:S(2)}) collective-permute-start(f32[128,256]{0,1:T(8,128)S(1)} %get-tuple-element.126), channel_id=1, source_target_pairs={{0,8},{1,12},{2,0},{3,4},{4,24},{5,28},{6,16},{7,20},{8,9},{9,13},... | collective-permute-start | bytes 393224 | tf_op jit(solution)/shard_map/ppermute | solution.py:163
  121.6 2.1 collective-permute-start.22
  123.8 1.9 collective-permute-start.27
  125.8 2.4 %collective-permute-done.22 = f32[128,256]{0,1:T(8,128)S(1)} collective-permute-done((f32[128,256]{0,1:T(8,128)S(1)}, f32[128,256]{0,1:T(8,128)S(1)}, u32[]{:S(2)}, u32[]{:S(2)}) %collective-permute-start.22) | collective-permute-done | bytes 131104 | tf_op jit(solution)/shard_map/ppermute | solution.py:163
  128.2 1.7 collective-permute-start.23
  131.7 8.7 %shard_map.133 = (bf16[768,2048]{1,0:T(8,128)(2,1)S(1)}, bf16[768,2048]{1,0:T(8,128)(2,1)S(1)}) custom-call(f32[768,8]{1,0:T(8,128)S(1)} %bitcast.158, f32[8,2048]{1,0:T(8,128)S(1)} %copy-done.2), custom_call_target="tpu_custom_call" | custom-call | flops 6291456000 | bytes 6291456 | tf_op jit(solution)/shard_map/pallas_call | solution.py:61
  140.5 2.2 %collective-permute-start.29 = (f32[512,256]{1,0:T(8,128)S(1)}, f32[512,256]{1,0:T(8,128)S(1)}, u32[]{:S(2)}, u32[]{:S(2)}) collective-permute-start(f32[512,256]{1,0:T(8,128)S(1)} %constant_dynamic-slice_fusion.1), channel_id=1, source_target_pairs={{3,0},{0,1},{1,2},{2,3},{7,4},{4,5},{5,6},{6,7},{11,8},{8,9},{9,10... | collective-permute-start | bytes 1572872 | tf_op jit(solution)/shard_map/ppermute | solution.py:138
  142.9 8.3 %collective-permute-start.26 = (f32[4,128,256]{1,2,0:T(8,128)S(1)}, f32[4,128,256]{1,2,0:T(8,128)S(1)}, u32[]{:S(2)}, u32[]{:S(2)}) collective-permute-start(f32[4,128,256]{1,2,0:T(8,128)S(1)} %constant_dynamic-slice_fusion.2), channel_id=1, source_target_pairs={{0,4},{4,0},{8,12},{12,8},{16,20},{20,16},{24,28},{28,24},{1,5},{5... | collective-permute-start | bytes 1572872 | tf_op jit(solution)/shard_map/ppermute | solution.py:145
  152.4 6.4 %collective-permute-start.30 = (f32[3,512,256]{2,1,0:T(8,128)}, f32[3,512,256]{2,1,0:T(8,128)}, u32[]{:S(2)}, u32[]{:S(2)}) collective-permute-start(f32[3,512,256]{2,1,0:T(8,128)} %pad_maximum_fusion.4), channel_id=1, source_target_pairs={{0,4},{4,0},{8,12},{12,8},{16,20},{20,16},{24,28},{28,24},{1,5},{5... | collective-permute-start | bytes 4718600 | tf_op jit(solution)/shard_map/ppermute | solution.py:145
  160.0 2.5 %copy.73 = f32[4,2,128,256]{3,2,1,0:T(8,128)} copy(f32[4,2,128,256]{2,3,0,1:T(8,128)} %pad_maximum_fusion.8) | data formatting | bytes 2097152 | tf_op jit(solution)/shard_map/stack | solution.py:150
  162.5 1.9 constant_dynamic-slice_fusion
  165.6 2.2 %collective-permute-start.32 = (f32[512,256]{1,0:T(8,128)}, f32[512,256]{1,0:T(8,128)}, u32[]{:S(2)}, u32[]{:S(2)}) collective-permute-start(f32[512,256]{1,0:T(8,128)} %constant_dynamic-slice_fusion), channel_id=1, source_target_pairs={{2,0},{3,1},{0,2},{1,3},{6,4},{7,5},{4,6},{5,7},{10,8},{11,9},{8,1... | collective-permute-start | bytes 1572872 | tf_op jit(solution)/shard_map/ppermute | solution.py:138
  168.6 8.7 %shard_map.134 = (bf16[768,2048]{1,0:T(8,128)(2,1)S(1)}, bf16[768,2048]{1,0:T(8,128)(2,1)S(1)}) custom-call(f32[768,8]{1,0:T(8,128)S(1)} %bitcast.159, f32[8,2048]{1,0:T(8,128)S(1)} %copy-done.3), custom_call_target="tpu_custom_call" | custom-call | flops 6291456000 | bytes 6291456 | tf_op jit(solution)/shard_map/pallas_call | solution.py:61
  177.3 1.6 copy-done.12
  179.0 1.7 copy-done.14
  180.7 2.7 %stack.181 = f32[1,1024,2,128]{3,2,1,0:T(2,128)} reshape(f32[1024,256]{1,0:T(8,128)} %bitcast.163) | data formatting | bytes 2097152 | tf_op jit(solution)/shard_map/stack | solution.py:247
  183.4 2.3 %copy.74 = f32[1,1024,2,128]{3,1,2,0:T(8,128)} copy(f32[1,1024,2,128]{3,2,1,0:T(2,128)} %stack.181) | data formatting | bytes 2097152 | tf_op jit(solution)/shard_map/stack | solution.py:247
  185.7 2.7 %stack.182 = f32[1,1024,2,128]{3,2,1,0:T(2,128)} reshape(f32[1024,256]{1,0:T(8,128)} %bitcast.166) | data formatting | bytes 2097152 | tf_op jit(solution)/shard_map/stack | solution.py:247
  189.7 2.7 %maximum_bitcast_fusion = f32[2,2,1024,128]{3,2,1,0:T(8,128)} fusion(f32[1,1024,2,128]{3,1,2,0:T(8,128)S(1)} %copy.75, f32[1,1024,2,128]{3,1,2,0:T(8,128)} %copy.74), kind=kLoop, calls=%fused_computation.4 | loop fusion | flops 524288 | bytes 4194304 | tf_op jit(solution)/shard_map/transpose | solution.py:249
  192.4 2.2 %select_bitcast_fusion.3 = (f32[3,1,512,256]{3,2,0,1:T(8,128)S(1)}, f32[3,1,512,256]{3,2,0,1:T(8,128)S(1)}) fusion(f32[3,512,256]{2,1,0:T(8,128)} %pad_maximum_fusion.4, f32[3,512,256]{2,1,0:T(8,128)} %collective-permute-done.30, pred[]{:T(512)S(6)} %eq.36), kind=kLoop, calls=%fused_computation.28 | loop fusion | flops 786432 | bytes 6291457 | tf_op jit(solution)/shard_map/stack | solution.py:150
  (187 shorter events, 48.9 us)
Async XLA Ops:
  6.5 18.9 %copy-start.27 = (f32[2,2]{1,0:T(2,128)S(1)}, f32[2,2]{1,0:T(2,128)}, u32[]{:S(2)}) copy-start(f32[2,2]{1,0:T(2,128)} %param.22) | copy-start | bytes 52
  6.5 20.2 %copy-start.25 = (f32[2,1024]{1,0:T(2,128)S(1)}, f32[2,1024]{1,0:T(2,128)}, u32[]{:S(2)}) copy-start(f32[2,1024]{1,0:T(2,128)} %param.18) | copy-start | bytes 24580
  6.5 20.2 %copy-start.26 = (s32[2,1024]{1,0:T(2,128)S(1)}, s32[2,1024]{1,0:T(2,128)}, u32[]{:S(2)}) copy-start(s32[2,1024]{1,0:T(2,128)} %param.19) | copy-start | bytes 24580
  6.6 22.8 %copy-start.24 = (f32[2,2,1024]{2,1,0:T(2,128)S(1)}, f32[2,2,1024]{2,1,0:T(2,128)}, u32[]{:S(2)}) copy-start(f32[2,2,1024]{2,1,0:T(2,128)} %param.17) | copy-start | bytes 49156
  10.1 25.3 %collective-permute-start = (f32[128,256]{0,1:T(8,128)S(1)}, f32[128,256]{0,1:T(8,128)S(1)}, u32[]{:S(2)}, u32[]{:S(2)}) collective-permute-start(f32[128,256]{0,1:T(8,128)S(1)} %get-tuple-element.137), channel_id=1, source_target_pairs={{0,0},{1,4},{2,8},{3,12},{4,16},{5,20},{6,24},{7,28},{8,1},{9,5},{... | collective-permute-start | bytes 393224 | tf_op jit(solution)/shard_map/ppermute | solution.py:163
  15.7 19.7 %collective-permute-start.1 = (f32[128,256]{0,1:T(8,128)S(1)}, f32[128,256]{0,1:T(8,128)S(1)}, u32[]{:S(2)}, u32[]{:S(2)}) collective-permute-start(f32[128,256]{0,1:T(8,128)S(1)} %get-tuple-element.134), channel_id=1, source_target_pairs={{0,4},{1,8},{2,12},{3,0},{4,20},{5,24},{6,28},{7,16},{8,5},{9,9},{... | collective-permute-start | bytes 393224 | tf_op jit(solution)/shard_map/ppermute | solution.py:163
  18.9 16.6 %collective-permute-start.2 = (f32[128,256]{0,1:T(8,128)S(1)}, f32[128,256]{0,1:T(8,128)S(1)}, u32[]{:S(2)}, u32[]{:S(2)}) collective-permute-start(f32[128,256]{0,1:T(8,128)S(1)} %get-tuple-element.136), channel_id=1, source_target_pairs={{0,8},{1,12},{2,0},{3,4},{4,24},{5,28},{6,16},{7,20},{8,9},{9,13},... | collective-permute-start | bytes 393224 | tf_op jit(solution)/shard_map/ppermute | solution.py:163
  23.5 12.0 %collective-permute-start.3 = (f32[128,256]{0,1:T(8,128)S(1)}, f32[128,256]{0,1:T(8,128)S(1)}, u32[]{:S(2)}, u32[]{:S(2)}) collective-permute-start(f32[128,256]{0,1:T(8,128)S(1)} %get-tuple-element.135), channel_id=1, source_target_pairs={{0,12},{1,0},{2,4},{3,8},{4,28},{5,16},{6,20},{7,24},{8,13},{9,1},... | collective-permute-start | bytes 393224 | tf_op jit(solution)/shard_map/ppermute | solution.py:163
  30.1 3.9 %collective-permute-start.4 = (f32[8,2,1024]{2,0,1:T(8,128)}, f32[8,2,1024]{2,0,1:T(8,128)S(1)}, u32[]{:S(2)}, u32[]{:S(2)}) collective-permute-start(f32[8,2,1024]{2,0,1:T(8,128)} %stack.156), channel_id=1, source_target_pairs={{1,0},{2,1},{3,2},{0,3},{5,4},{6,5},{7,6},{4,7},{9,8},{10,9},{11,1... | collective-permute-start | bytes 196616 | tf_op jit(solution)/shard_map/ppermute | solution.py:138
  35.5 13.6 %collective-permute-start.5 = (f32[128,256]{0,1:T(8,128)S(1)}, f32[128,256]{0,1:T(8,128)S(1)}, u32[]{:S(2)}, u32[]{:S(2)}) collective-permute-start(f32[128,256]{0,1:T(8,128)S(1)} %add_add_fusion.2), channel_id=1, source_target_pairs={{8,0},{12,4},{16,8},{20,12},{24,16},{28,20},{0,24},{4,28},{9,1},{1... | collective-permute-start | bytes 393224 | tf_op jit(solution)/shard_map/ppermute | solution.py:142
  36.7 12.4 %collective-permute-start.6 = (f32[128,256]{0,1:T(8,128)S(1)}, f32[128,256]{0,1:T(8,128)S(1)}, u32[]{:S(2)}, u32[]{:S(2)}) collective-permute-start(f32[128,256]{0,1:T(8,128)S(1)} %add_add_fusion.2), channel_id=1, source_target_pairs={{16,0},{20,4},{24,8},{28,12},{0,16},{4,20},{8,24},{12,28},{17,1},{... | collective-permute-start | bytes 393224 | tf_op jit(solution)/shard_map/ppermute | solution.py:142
  36.7 12.4 %collective-permute-start.7 = (f32[128,256]{0,1:T(8,128)S(1)}, f32[128,256]{0,1:T(8,128)S(1)}, u32[]{:S(2)}, u32[]{:S(2)}) collective-permute-start(f32[128,256]{0,1:T(8,128)S(1)} %add_add_fusion.2), channel_id=1, source_target_pairs={{24,0},{28,4},{0,8},{4,12},{8,16},{12,20},{16,24},{20,28},{25,1},{... | collective-permute-start | bytes 393224 | tf_op jit(solution)/shard_map/ppermute | solution.py:142
  49.1 5.1 %copy-start.21 = (f32[2,512,128]{2,1,0:T(8,128)S(1)}, f32[2,512,128]{2,1,0:T(8,128)}, u32[]{:S(2)}) copy-start(f32[2,512,128]{2,1,0:T(8,128)} %param.16) | copy-start | bytes 1572868
  49.3 9.3 %collective-permute-start.8 = (f32[4,128,256]{1,2,0:T(8,128)S(1)}, f32[4,128,256]{1,2,0:T(8,128)S(1)}, u32[]{:S(2)}, u32[]{:S(2)}) collective-permute-start(f32[4,128,256]{1,2,0:T(8,128)S(1)} %constant_dynamic-slice_fusion.8), channel_id=1, source_target_pairs={{0,4},{4,0},{8,12},{12,8},{16,20},{20,16},{24,28},{28,24},{1,5},{5... | collective-permute-start | bytes 1572872 | tf_op jit(solution)/shard_map/ppermute | solution.py:145
  51.7 4.5 %collective-permute-start.13 = (f32[8,2,1024]{2,0,1:T(8,128)}, f32[8,2,1024]{2,0,1:T(8,128)}, u32[]{:S(2)}, u32[]{:S(2)}) collective-permute-start(f32[8,2,1024]{2,0,1:T(8,128)} %stack.156), channel_id=1, source_target_pairs={{2,0},{3,1},{0,2},{1,3},{6,4},{7,5},{4,6},{5,7},{10,8},{11,9},{8,1... | collective-permute-start | bytes 196616 | tf_op jit(solution)/shard_map/ppermute | solution.py:138
  53.5 4.3 %collective-permute-start.14 = (f32[8,2,1024]{2,0,1:T(8,128)}, f32[8,2,1024]{2,0,1:T(8,128)}, u32[]{:S(2)}, u32[]{:S(2)}) collective-permute-start(f32[8,2,1024]{2,0,1:T(8,128)} %stack.156), channel_id=1, source_target_pairs={{3,0},{0,1},{1,2},{2,3},{7,4},{4,5},{5,6},{6,7},{11,8},{8,9},{9,10... | collective-permute-start | bytes 196616 | tf_op jit(solution)/shard_map/ppermute | solution.py:138
  59.7 64.0 %copy-start.16 = (f32[4,2,128,256]{3,2,1,0:T(8,128)}, f32[4,2,128,256]{3,2,1,0:T(8,128)S(1)}, u32[]{:S(2)}) copy-start(f32[4,2,128,256]{3,2,1,0:T(8,128)S(1)} %copy.69) | copy-start | bytes 3145732
  59.7 4.1 %copy-start.19 = (f32[2,512,1024]{2,1,0:T(8,128)S(1)}, f32[2,512,1024]{2,1,0:T(8,128)}, u32[]{:S(2)}) copy-start(f32[2,512,1024]{2,1,0:T(8,128)} %param.14) | copy-start | bytes 12582916
  63.8 16.2 %copy-start.23 = (f32[8,2,2048]{2,0,1:T(8,128)S(1)}, f32[8,2,2048]{2,0,1:T(8,128)}, u32[]{:S(2)}) copy-start(f32[8,2,2048]{2,0,1:T(8,128)} %copy-done.22) | copy-start | bytes 393220
  65.9 14.8 %collective-permute-start.10 = (f32[128,256]{0,1:T(8,128)S(1)}, f32[128,256]{0,1:T(8,128)S(1)}, u32[]{:S(2)}, u32[]{:S(2)}) collective-permute-start(f32[128,256]{0,1:T(8,128)S(1)} %get-tuple-element.128), channel_id=1, source_target_pairs={{0,4},{1,8},{2,12},{3,0},{4,20},{5,24},{6,28},{7,16},{8,5},{9,9},{... | collective-permute-start | bytes 393224 | tf_op jit(solution)/shard_map/ppermute | solution.py:163
  69.4 11.3 %collective-permute-start.11 = (f32[128,256]{0,1:T(8,128)S(1)}, f32[128,256]{0,1:T(8,128)S(1)}, u32[]{:S(2)}, u32[]{:S(2)}) collective-permute-start(f32[128,256]{0,1:T(8,128)S(1)} %get-tuple-element.130), channel_id=1, source_target_pairs={{0,8},{1,12},{2,0},{3,4},{4,24},{5,28},{6,16},{7,20},{8,9},{9,13},... | collective-permute-start | bytes 393224 | tf_op jit(solution)/shard_map/ppermute | solution.py:163
  72.1 8.6 %collective-permute-start.12 = (f32[128,256]{0,1:T(8,128)S(1)}, f32[128,256]{0,1:T(8,128)S(1)}, u32[]{:S(2)}, u32[]{:S(2)}) collective-permute-start(f32[128,256]{0,1:T(8,128)S(1)} %get-tuple-element.129), channel_id=1, source_target_pairs={{0,12},{1,0},{2,4},{3,8},{4,28},{5,16},{6,20},{7,24},{8,13},{9,1},... | collective-permute-start | bytes 393224 | tf_op jit(solution)/shard_map/ppermute | solution.py:163
  75.0 7.0 %collective-permute-start.9 = (f32[128,256]{0,1:T(8,128)S(1)}, f32[128,256]{0,1:T(8,128)S(1)}, u32[]{:S(2)}, u32[]{:S(2)}) collective-permute-start(f32[128,256]{0,1:T(8,128)S(1)} %get-tuple-element.131), channel_id=1, source_target_pairs={{0,0},{1,4},{2,8},{3,12},{4,16},{5,20},{6,24},{7,28},{8,1},{9,5},{... | collective-permute-start | bytes 393224 | tf_op jit(solution)/shard_map/ppermute | solution.py:163
  82.0 17.4 %collective-permute-start.15 = (f32[128,256]{0,1:T(8,128)S(1)}, f32[128,256]{0,1:T(8,128)S(1)}, u32[]{:S(2)}, u32[]{:S(2)}) collective-permute-start(f32[128,256]{0,1:T(8,128)S(1)} %add_add_fusion.1), channel_id=1, source_target_pairs={{8,0},{12,4},{16,8},{20,12},{24,16},{28,20},{0,24},{4,28},{9,1},{1... | collective-permute-start | bytes 393224 | tf_op jit(solution)/shard_map/ppermute | solution.py:142
  86.9 12.5 %collective-permute-start.16 = (f32[128,256]{0,1:T(8,128)S(1)}, f32[128,256]{0,1:T(8,128)S(1)}, u32[]{:S(2)}, u32[]{:S(2)}) collective-permute-start(f32[128,256]{0,1:T(8,128)S(1)} %add_add_fusion.1), channel_id=1, source_target_pairs={{16,0},{20,4},{24,8},{28,12},{0,16},{4,20},{8,24},{12,28},{17,1},{... | collective-permute-start | bytes 393224 | tf_op jit(solution)/shard_map/ppermute | solution.py:142
  87.0 12.5 %collective-permute-start.17 = (f32[128,256]{0,1:T(8,128)S(1)}, f32[128,256]{0,1:T(8,128)S(1)}, u32[]{:S(2)}, u32[]{:S(2)}) collective-permute-start(f32[128,256]{0,1:T(8,128)S(1)} %add_add_fusion.1), channel_id=1, source_target_pairs={{24,0},{28,4},{0,8},{4,12},{8,16},{12,20},{16,24},{20,28},{25,1},{... | collective-permute-start | bytes 393224 | tf_op jit(solution)/shard_map/ppermute | solution.py:142
  99.7 3.5 %collective-permute-start.18 = (f32[4,128,256]{1,2,0:T(8,128)S(1)}, f32[4,128,256]{1,2,0:T(8,128)S(1)}, u32[]{:S(2)}, u32[]{:S(2)}) collective-permute-start(f32[4,128,256]{1,2,0:T(8,128)S(1)} %constant_dynamic-slice_fusion.3), channel_id=1, source_target_pairs={{0,4},{4,0},{8,12},{12,8},{16,20},{20,16},{24,28},{28,24},{1,5},{5... | collective-permute-start | bytes 1572872 | tf_op jit(solution)/shard_map/ppermute | solution.py:145
  103.6 3.8 %copy-start.20 = (f32[2,512,1024]{2,1,0:T(8,128)S(1)}, f32[2,512,1024]{2,1,0:T(8,128)}, u32[]{:S(2)}) copy-start(f32[2,512,1024]{2,1,0:T(8,128)} %param.13) | copy-start | bytes 12582916
  109.5 16.3 %collective-permute-start.19 = (f32[128,256]{0,1:T(8,128)S(1)}, f32[128,256]{0,1:T(8,128)S(1)}, u32[]{:S(2)}, u32[]{:S(2)}) collective-permute-start(f32[128,256]{0,1:T(8,128)S(1)} %get-tuple-element.127), channel_id=1, source_target_pairs={{0,0},{1,4},{2,8},{3,12},{4,16},{5,20},{6,24},{7,28},{8,1},{9,5},{... | collective-permute-start | bytes 393224 | tf_op jit(solution)/shard_map/ppermute | solution.py:163
  113.7 12.1 %collective-permute-start.20 = (f32[128,256]{0,1:T(8,128)S(1)}, f32[128,256]{0,1:T(8,128)S(1)}, u32[]{:S(2)}, u32[]{:S(2)}) collective-permute-start(f32[128,256]{0,1:T(8,128)S(1)} %get-tuple-element.124), channel_id=1, source_target_pairs={{0,4},{1,8},{2,12},{3,0},{4,20},{5,24},{6,28},{7,16},{8,5},{9,9},{... | collective-permute-start | bytes 393224 | tf_op jit(solution)/shard_map/ppermute | solution.py:163
  117.1 8.6 %collective-permute-start.21 = (f32[128,256]{0,1:T(8,128)S(1)}, f32[128,256]{0,1:T(8,128)S(1)}, u32[]{:S(2)}, u32[]{:S(2)}) collective-permute-start(f32[128,256]{0,1:T(8,128)S(1)} %get-tuple-element.126), channel_id=1, source_target_pairs={{0,8},{1,12},{2,0},{3,4},{4,24},{5,28},{6,16},{7,20},{8,9},{9,13},... | collective-permute-start | bytes 393224 | tf_op jit(solution)/shard_map/ppermute | solution.py:163
  121.6 6.6 %collective-permute-start.22 = (f32[128,256]{0,1:T(8,128)S(1)}, f32[128,256]{0,1:T(8,128)S(1)}, u32[]{:S(2)}, u32[]{:S(2)}) collective-permute-start(f32[128,256]{0,1:T(8,128)S(1)} %get-tuple-element.125), channel_id=1, source_target_pairs={{0,12},{1,0},{2,4},{3,8},{4,28},{5,16},{6,20},{7,24},{8,13},{9,1},... | collective-permute-start | bytes 393224 | tf_op jit(solution)/shard_map/ppermute | solution.py:163
  123.8 27.3 %collective-permute-start.27 = (f32[512,256]{1,0:T(8,128)S(1)}, f32[512,256]{1,0:T(8,128)S(1)}, u32[]{:S(2)}, u32[]{:S(2)}) collective-permute-start(f32[512,256]{1,0:T(8,128)S(1)} %constant_dynamic-slice_fusion.1), channel_id=1, source_target_pairs={{1,0},{2,1},{3,2},{0,3},{5,4},{6,5},{7,6},{4,7},{9,8},{10,9},{11,1... | collective-permute-start | bytes 1572872 | tf_op jit(solution)/shard_map/ppermute | solution.py:138
  125.8 25.4 %collective-permute-start.28 = (f32[512,256]{1,0:T(8,128)S(1)}, f32[512,256]{1,0:T(8,128)S(1)}, u32[]{:S(2)}, u32[]{:S(2)}) collective-permute-start(f32[512,256]{1,0:T(8,128)S(1)} %constant_dynamic-slice_fusion.1), channel_id=1, source_target_pairs={{2,0},{3,1},{0,2},{1,3},{6,4},{7,5},{4,6},{5,7},{10,8},{11,9},{8,1... | collective-permute-start | bytes 1572872 | tf_op jit(solution)/shard_map/ppermute | solution.py:138
  128.2 12.2 %collective-permute-start.23 = (f32[128,256]{0,1:T(8,128)S(1)}, f32[128,256]{0,1:T(8,128)S(1)}, u32[]{:S(2)}, u32[]{:S(2)}) collective-permute-start(f32[128,256]{0,1:T(8,128)S(1)} %add_add_fusion), channel_id=1, source_target_pairs={{8,0},{12,4},{16,8},{20,12},{24,16},{28,20},{0,24},{4,28},{9,1},{1... | collective-permute-start | bytes 393224 | tf_op jit(solution)/shard_map/ppermute | solution.py:142
  130.0 12.7 %collective-permute-start.24 = (f32[128,256]{0,1:T(8,128)S(1)}, f32[128,256]{0,1:T(8,128)S(1)}, u32[]{:S(2)}, u32[]{:S(2)}) collective-permute-start(f32[128,256]{0,1:T(8,128)S(1)} %add_add_fusion), channel_id=1, source_target_pairs={{16,0},{20,4},{24,8},{28,12},{0,16},{4,20},{8,24},{12,28},{17,1},{... | collective-permute-start | bytes 393224 | tf_op jit(solution)/shard_map/ppermute | solution.py:142
  130.0 12.7 %collective-permute-start.25 = (f32[128,256]{0,1:T(8,128)S(1)}, f32[128,256]{0,1:T(8,128)S(1)}, u32[]{:S(2)}, u32[]{:S(2)}) collective-permute-start(f32[128,256]{0,1:T(8,128)S(1)} %add_add_fusion), channel_id=1, source_target_pairs={{24,0},{28,4},{0,8},{4,12},{8,16},{12,20},{16,24},{20,28},{25,1},{... | collective-permute-start | bytes 393224 | tf_op jit(solution)/shard_map/ppermute | solution.py:142
  140.4 12.0 %copy-start.10 = (bf16[768,2048]{1,0:T(8,128)(2,1)}, bf16[768,2048]{1,0:T(8,128)(2,1)S(1)}, u32[]{:S(2)}) copy-start(bf16[768,2048]{1,0:T(8,128)(2,1)S(1)} %get-tuple-element.96) | copy-start | bytes 9437188
  140.5 10.7 %collective-permute-start.29 = (f32[512,256]{1,0:T(8,128)S(1)}, f32[512,256]{1,0:T(8,128)S(1)}, u32[]{:S(2)}, u32[]{:S(2)}) collective-permute-start(f32[512,256]{1,0:T(8,128)S(1)} %constant_dynamic-slice_fusion.1), channel_id=1, source_target_pairs={{3,0},{0,1},{1,2},{2,3},{7,4},{4,5},{5,6},{6,7},{11,8},{8,9},{9,10... | collective-permute-start | bytes 1572872 | tf_op jit(solution)/shard_map/ppermute | solution.py:138
  142.9 16.0 %collective-permute-start.26 = (f32[4,128,256]{1,2,0:T(8,128)S(1)}, f32[4,128,256]{1,2,0:T(8,128)S(1)}, u32[]{:S(2)}, u32[]{:S(2)}) collective-permute-start(f32[4,128,256]{1,2,0:T(8,128)S(1)} %constant_dynamic-slice_fusion.2), channel_id=1, source_target_pairs={{0,4},{4,0},{8,12},{12,8},{16,20},{20,16},{24,28},{28,24},{1,5},{5... | collective-permute-start | bytes 1572872 | tf_op jit(solution)/shard_map/ppermute | solution.py:145
  152.4 40.0 %collective-permute-start.30 = (f32[3,512,256]{2,1,0:T(8,128)}, f32[3,512,256]{2,1,0:T(8,128)}, u32[]{:S(2)}, u32[]{:S(2)}) collective-permute-start(f32[3,512,256]{2,1,0:T(8,128)} %pad_maximum_fusion.4), channel_id=1, source_target_pairs={{0,4},{4,0},{8,12},{12,8},{16,20},{20,16},{24,28},{28,24},{1,5},{5... | collective-permute-start | bytes 4718600 | tf_op jit(solution)/shard_map/ppermute | solution.py:145
  164.4 31.0 %collective-permute-start.31 = (f32[512,256]{1,0:T(8,128)}, f32[512,256]{1,0:T(8,128)}, u32[]{:S(2)}, u32[]{:S(2)}) collective-permute-start(f32[512,256]{1,0:T(8,128)} %constant_dynamic-slice_fusion), channel_id=1, source_target_pairs={{1,0},{2,1},{3,2},{0,3},{5,4},{6,5},{7,6},{4,7},{9,8},{10,9},{11,1... | collective-permute-start | bytes 1572872 | tf_op jit(solution)/shard_map/ppermute | solution.py:138
  165.6 29.9 %collective-permute-start.32 = (f32[512,256]{1,0:T(8,128)}, f32[512,256]{1,0:T(8,128)}, u32[]{:S(2)}, u32[]{:S(2)}) collective-permute-start(f32[512,256]{1,0:T(8,128)} %constant_dynamic-slice_fusion), channel_id=1, source_target_pairs={{2,0},{3,1},{0,2},{1,3},{6,4},{7,5},{4,6},{5,7},{10,8},{11,9},{8,1... | collective-permute-start | bytes 1572872 | tf_op jit(solution)/shard_map/ppermute | solution.py:138
  167.8 27.7 %collective-permute-start.33 = (f32[512,256]{1,0:T(8,128)}, f32[512,256]{1,0:T(8,128)}, u32[]{:S(2)}, u32[]{:S(2)}) collective-permute-start(f32[512,256]{1,0:T(8,128)} %constant_dynamic-slice_fusion), channel_id=1, source_target_pairs={{3,0},{0,1},{1,2},{2,3},{7,4},{4,5},{5,6},{6,7},{11,8},{8,9},{9,10... | collective-permute-start | bytes 1572872 | tf_op jit(solution)/shard_map/ppermute | solution.py:138
  195.4 2.2 %copy-start.17 = (f32[4,2,128,256]{3,2,1,0:T(8,128)S(1)}, f32[4,2,128,256]{3,2,1,0:T(8,128)}, u32[]{:S(2)}) copy-start(f32[4,2,128,256]{3,2,1,0:T(8,128)} %copy-done.16) | copy-start | bytes 3145732
  197.0 6.9 %collective-permute-start.34 = (f32[3,512,256]{2,1,0:T(8,128)S(1)}, f32[3,512,256]{2,1,0:T(8,128)S(1)}, u32[]{:S(2)}, u32[]{:S(2)}) collective-permute-start(f32[3,512,256]{2,1,0:T(8,128)S(1)} %pad_maximum_fusion.5), channel_id=1, source_target_pairs={{0,4},{4,0},{8,12},{12,8},{16,20},{20,16},{24,28},{28,24},{1,5},{5... | collective-permute-start | bytes 4718600 | tf_op jit(solution)/shard_map/ppermute | solution.py:145
  198.6 2.3 %copy-start.9 = (bf16[768,2048]{1,0:T(8,128)(2,1)S(1)}, bf16[768,2048]{1,0:T(8,128)(2,1)}, u32[]{:S(2)}) copy-start(bf16[768,2048]{1,0:T(8,128)(2,1)} %copy-done.8) | copy-start | bytes 9437188
  207.1 2.1 copy-start.13
  (15 other events, 23.1 us)
